TPU v7x, 512 devices: a whole 4x8x8 slice. The times are simulated.
512 devices in a mesh: row: 64 (over z_hi, y, core), col: 8 (over x, z_lo).
Axes of the slice: x: 4, y: 8, z: 8 (z_hi: 4, z_lo: 2; z = z_hi * 2 + z_lo), core: 2. Of those that a mesh axis runs over, the one named last changes fastest.
Arguments:
- counts: int32 [49152, 9216], P('row', 'col'), may hold values from 0 to 63
- row_marg: int32 [49152], P('row'), may hold values from 1 to 24570
- col_marg: int32 [9216], P('col'), may hold values from 49152 to 3096576
- row_emb: float32 [300, 49152], P(None, ('row', 'col')), may hold values from -0.375 to 0.375
- col_emb: float32 [300, 9216], P(None, ('col', 'row')), may hold values from -0.375 to 0.375
- row_acc: float32 [300, 49152], P(None, ('row', 'col')), may hold values from 10 to 1000
- col_acc: float32 [300, 9216], P(None, ('col', 'row')), may hold values from 10 to 1000
Outputs:
- new_row_emb: float32 [300, 49152], P(None, ('row', 'col'))
- new_col_emb: float32 [300, 9216], P(None, ('col', 'row'))
- new_row_acc: float32 [300, 49152], P(None, ('row', 'col'))
- new_col_acc: float32 [300, 9216], P(None, ('col', 'row'))
All inputs are finite; a program needn't handle non-finite values.
Results may differ from a plain program's by a relative error of at most 0.0078.
Values may be sent and summed in bfloat16 or wider, within the bound.
No kernel may reach another device: no remote copies, remote signals or barrier semaphores. Data moves between devices by JAX's collectives and lax.ppermute only.
A program may use at most 64 MiB of HBM per device.

v0:
```python
import jax
import jax.numpy as jnp
from jax import lax
from jax.sharding import PartitionSpec as P


def cell_gradient(counts, row_log, col_log, log_total, scores):
    pmi_base = log_total - row_log[:, None] - col_log[None, :]
    count_float = counts.astype(jnp.float32)
    weight = 0.1 + 0.25 * jnp.sqrt(count_float)
    fitted = weight * (scores - pmi_base - jnp.log(jnp.maximum(count_float, 1.0)))
    return jnp.where(counts > 0, fitted, jax.nn.sigmoid(scores - pmi_base)).astype(jnp.bfloat16)


def adagrad(embedding, accumulator, gradient):
    new_acc = accumulator + gradient * gradient
    return (embedding - gradient / jnp.sqrt(new_acc), new_acc)


def body(counts, row_marg, col_marg, row_emb, col_emb, row_acc, col_acc):
    grand_total = lax.psum(jnp.sum(row_marg.astype(jnp.float32)), "row")
    log_total = jnp.log(grand_total)
    row_half = lax.all_gather(row_emb.astype(jnp.bfloat16), "col", axis=1, tiled=True)
    col_half = lax.all_gather(col_emb.astype(jnp.bfloat16), "row", axis=1, tiled=True)
    scores = lax.dot_general(
        row_half, col_half, (((0,), (0,)), ((), ())), preferred_element_type=jnp.float32
    )
    row_log = jnp.log(row_marg.astype(jnp.float32))
    col_log = jnp.log(col_marg.astype(jnp.float32))
    cell_slope = cell_gradient(counts, row_log, col_log, log_total, scores)
    row_grad = lax.dot_general(
        col_half, cell_slope, (((1,), (1,)), ((), ())), preferred_element_type=jnp.float32
    )
    col_grad = lax.dot_general(
        row_half, cell_slope, (((1,), (0,)), ((), ())), preferred_element_type=jnp.float32
    )
    row_share = lax.psum_scatter(row_grad, "col", scatter_dimension=1, tiled=True)
    col_share = lax.psum_scatter(col_grad, "row", scatter_dimension=1, tiled=True)
    new_row_emb, new_row_acc = adagrad(row_emb, row_acc, row_share)
    new_col_emb, new_col_acc = adagrad(col_emb, col_acc, col_share)
    return (new_row_emb, new_col_emb, new_row_acc, new_col_acc)


def solution(mesh):
    return jax.shard_map(
        body,
        mesh=mesh,
        in_specs=(
            P("row", "col"),
            P("row"),
            P("col"),
            P(None, ("row", "col")),
            P(None, ("col", "row")),
            P(None, ("row", "col")),
            P(None, ("col", "row")),
        ),
        out_specs=(
            P(None, ("row", "col")),
            P(None, ("col", "row")),
            P(None, ("row", "col")),
            P(None, ("col", "row")),
        ),
        check_vma=False,
    )
```

profile of v0, /device:TPU:4, one launch (start us, length us, event | category | flops | bytes accessed | tf_op | source)
XLA Modules:
  0.0 837.5 jit_solution(3822353473362909096)
XLA Ops:
  8.0 0.0 copy-start.5
  8.0 0.0 all-reduce.3.cloned.1.call-start
  8.1 0.8 convert_bitcast_fusion
  8.8 91.9 %all-gather = bf16[64,18,300]{2,1,0:T(8,128)(2,1)S(1)} all-gather(bf16[1,18,300]{2,1,0:T(8,128)(2,1)S(1)} %convert_bitcast_fusion), channel_id=1, replica_groups=mesh['row'=64,'col'=8] {'row'}, dimensions={0}, use_global_device_ids=true | all-gather | bytes 702000 | tf_op jit(solution)/shard_map/all_gather | solution.py:24
  100.7 0.9 convert_element_type.20
  101.7 26.9 %all_gather.6 = bf16[300,768]{0,1:T(8,128)(2,1)S(1)} all-gather(bf16[300,96]{0,1:T(8,128)(2,1)S(1)} %convert_element_type.20), channel_id=1, replica_groups=mesh['row'=64,'col'=8] {'col'}, dimensions={1}, use_global_device_ids=true | all-gather | bytes 518400 | tf_op jit(solution)/shard_map/all_gather | solution.py:23
  128.6 0.7 convert_log_fusion
  129.3 1.3 convert_reduce_fusion
  130.6 0.5 reshape.12
  131.1 0.0 copy-start
  131.1 139.1 %psum.7 = f32[]{:T(128)} all-reduce(f32[]{:T(128)} %convert_reduce_fusion), channel_id=1, replica_groups=mesh['row'=64,'col'=8] {'row'}, use_global_device_ids=true, to_apply=%region_1.0 | all-reduce | flops 1 | bytes 8 | tf_op jit(solution)/shard_map/psum | solution.py:21
  270.9 0.0 copy-done.5
  270.9 6.2 select_convert_fusion
  277.1 0.0 copy-done
  277.1 1.9 convolution_bitcast_fusion
  279.0 0.0 all-reduce.3.cloned.1.call-update
  279.1 0.0 copy-start.1
  279.1 0.0 copy-start.3
  279.1 0.0 copy-start.2
  279.1 0.0 copy-start.4
  279.1 0.0 reduce-scatter.5.cloned.1.call-start
  279.2 2.1 convolution_bitcast_fusion.1
  281.2 1.4 copy.35
  282.6 0.0 reduce-scatter.5.cloned.1.call-update
  282.6 0.0 copy-done.1
  282.6 0.1 copy.28
  282.7 0.0 copy-done.3
  282.7 0.1 copy.30
  282.9 0.0 copy-done.2
  282.9 0.1 copy.27
  283.0 0.0 copy-done.4
  283.0 0.1 copy.29
  283.1 1.3 dynamic-slice
  285.0 539.8 %all-reduce.3.cloned.1.call-done = f32[300,1152]{1,0:T(8,128)} async-done(((f32[300,1152]{1,0:T(8,128)}), f32[300,1152]{1,0:T(8,128)}) %all-reduce.3.cloned.1.call-update) | async-done | bytes 1382416
  824.9 1.1 multiply_subtract_fusion
  826.0 0.7 copy.32
  826.7 0.7 copy.34
  827.4 0.0 reduce-scatter.5.cloned.1.call-done
  827.4 1.0 copy.36
  828.5 0.8 copy.31
  829.3 0.8 copy.33
  (2 shorter events, 0.0 us)
Async XLA Ops:
  8.0 262.9 %copy-start.5 = (s32[768]{0:T(1024)S(1)}, s32[768]{0:T(1024)}, u32[]{:S(2)}) copy-start(s32[768]{0:T(1024)} %param.8) | copy-start | bytes 9220
  8.0 816.9 %all-reduce.3.cloned.1.call-start = ((), (), s32[]{:S(2)}) async-start(), calls=%async_computation.2 | async-start | bytes 2801664
  131.1 146.0 %copy-start = (bf16[1152,300]{1,0:T(8,128)(2,1)}, bf16[1152,300]{1,0:T(8,128)(2,1)S(1)}, u32[]{:S(2)}) copy-start(bf16[1152,300]{1,0:T(8,128)(2,1)S(1)} %reshape.12) | copy-start | bytes 2073604
  279.1 3.6 copy-start.1
  279.1 3.7 copy-start.3
  279.1 3.8 copy-start.2
  279.1 3.9 copy-start.4
  279.1 548.3 %reduce-scatter.5.cloned.1.call-start = ((), (), s32[]{:S(2)}) async-start(), calls=%async_computation.1 | async-start | bytes 1327104
Sparse Core Ops, SparseCore 0:
  279.2 545.6 all-reduce.2
Sparse Core Ops, SparseCore 1:
  282.7 39.5 reduce-scatter.4
where the time goes:
time: 838 us; the launch traced here: 837 us
  waiting for transfers between devices  540 us (64%)
  blocking collectives  258 us (31%)
  between operations  17 us (2%)
  matrix products  10.2 us (1%)
    unnamed x4, waiting for transfers between devices  540 us
    psum x1, blocking collectives, body(): grand_total = lax.psum(jnp.sum(row_marg.astype(jnp.float32)), 'row')  139 us
    all_gather x1, blocking collectives, body(): lax.all_gather(col_emb.astype(jnp.bfloat16), 'row', axis=1, tiled=True)  91.9 us
    all_gather x1, blocking collectives, body(): lax.all_gather(row_emb.astype(jnp.bfloat16), 'col', axis=1, tiled=True)  26.9 us
  transfers between devices with their start and end apart: 2, of which 1 were waited for; matrix products, arithmetic and copies ran while one was open for 1% of the time, Pallas kernels for 0%

commit v1 on v0

v1 whole, which is shorter than its diff:
```python
import jax
import jax.numpy as jnp
from jax import lax
from jax.sharding import Mesh, PartitionSpec as P

ROW_AXES = ("zh", "y", "core")
COL_AXES = ("x", "zl")
CHIP_AXES = ("zh", "y")


def cell_gradient(counts, row_log, col_log, log_total, scores):
    pmi_base = log_total - row_log[:, None] - col_log[None, :]
    count_float = counts.astype(jnp.float32)
    weight = 0.1 + 0.25 * jnp.sqrt(count_float)
    fitted = weight * (scores - pmi_base - jnp.log(jnp.maximum(count_float, 1.0)))
    return jnp.where(counts > 0, fitted, jax.nn.sigmoid(scores - pmi_base)).astype(jnp.bfloat16)


def adagrad(embedding, accumulator, gradient):
    new_acc = accumulator + gradient * gradient
    return (embedding - gradient / jnp.sqrt(new_acc), new_acc)


def split3(value):
    high = lax.reduce_precision(value, 8, 7)
    middle = lax.reduce_precision(value - high, 8, 7)
    low = lax.reduce_precision(value - high - middle, 8, 7)
    return jnp.stack([high, middle, low]).astype(jnp.bfloat16)


def exchange(blocks, axes):
    return lax.all_to_all(blocks, axes, 0, 0, tiled=True)


def swap(block):
    return lax.ppermute(block, "core", [(0, 1), (1, 0)])


def body(counts, row_marg, col_marg, row_emb, col_emb, row_acc, col_acc):
    n_col = lax.axis_size(COL_AXES)
    n_chip = lax.axis_size(CHIP_AXES)
    core = lax.axis_index("core")
    rows, cols = counts.shape
    depth, own_cols = col_emb.shape

    row_own = row_emb.T.astype(jnp.bfloat16)
    col_own = col_emb.T.astype(jnp.bfloat16)
    local_total = jnp.sum(row_marg).astype(jnp.float32)
    extra = jnp.zeros((1, depth), jnp.bfloat16).at[0, :3].set(split3(local_total))
    packed = jnp.concatenate([col_own, extra], axis=0)

    mine = exchange(jnp.broadcast_to(packed[None], (n_chip,) + packed.shape), CHIP_AXES)
    row_half = exchange(jnp.broadcast_to(row_own[None], (n_col,) + row_own.shape), COL_AXES)
    row_half = row_half.reshape(rows, depth)
    other = swap(mine)
    first = jnp.where(core == 0, mine, other)
    second = jnp.where(core == 0, other, mine)
    both = jnp.stack([first, second], axis=1)
    col_half = both[:, :, :own_cols].reshape(cols, depth)
    log_total = jnp.log(jnp.sum(both[:, :, own_cols, :3].astype(jnp.float32)))

    scores = lax.dot_general(
        row_half, col_half, (((1,), (1,)), ((), ())), preferred_element_type=jnp.float32
    )
    row_log = jnp.log(row_marg.astype(jnp.float32))
    col_log = jnp.log(col_marg.astype(jnp.float32))
    cell_slope = cell_gradient(counts, row_log, col_log, log_total, scores)
    col_grad = lax.dot_general(
        cell_slope, row_half, (((0,), (0,)), ((), ())), preferred_element_type=jnp.float32
    )
    row_grad = lax.dot_general(
        cell_slope, col_half, (((1,), (0,)), ((), ())), preferred_element_type=jnp.float32
    )

    col_parts = col_grad.astype(jnp.bfloat16).reshape(n_chip, 2, own_cols, depth)
    keep = jnp.where(core == 0, col_parts[:, 0], col_parts[:, 1])
    give = jnp.where(core == 0, col_parts[:, 1], col_parts[:, 0])
    pair = (keep.astype(jnp.float32) + swap(give).astype(jnp.float32)).astype(jnp.bfloat16)
    col_share = jnp.sum(exchange(pair, CHIP_AXES).astype(jnp.float32), axis=0)
    row_parts = row_grad.astype(jnp.bfloat16).reshape(n_col, rows // n_col, depth)
    row_share = jnp.sum(exchange(row_parts, COL_AXES).astype(jnp.float32), axis=0)

    new_row_emb, new_row_acc = adagrad(row_emb.T, row_acc.T, row_share)
    new_col_emb, new_col_acc = adagrad(col_emb.T, col_acc.T, col_share)
    return (new_row_emb.T, new_col_emb.T, new_row_acc.T, new_col_acc.T)


def solution(mesh):
    fine = Mesh(mesh.devices.reshape(4, 8, 2, 4, 2), ("zh", "y", "core", "x", "zl"))
    return jax.shard_map(
        body,
        mesh=fine,
        in_specs=(
            P(ROW_AXES, COL_AXES),
            P(ROW_AXES),
            P(COL_AXES),
            P(None, ROW_AXES + COL_AXES),
            P(None, COL_AXES + ROW_AXES),
            P(None, ROW_AXES + COL_AXES),
            P(None, COL_AXES + ROW_AXES),
        ),
        out_specs=(
            P(None, ROW_AXES + COL_AXES),
            P(None, COL_AXES + ROW_AXES),
            P(None, ROW_AXES + COL_AXES),
            P(None, COL_AXES + ROW_AXES),
        ),
        check_vma=False,
    )
```

time: 838 us -> 119 us (0.14)
  the two profiles are of different devices: /device:TPU:4 before, /device:TPU:8 now
where the time goes in v1:
time: 119 us; the launch traced here: 118 us
  blocking collectives  37.5 us (32%)
  waiting for transfers between devices  28.1 us (24%)
  starting transfers between devices  17.5 us (15%)
  local copies, waits for them, and re-layouts  11.9 us (10%)
  matrix products  8.59 us (7%)
  other arithmetic  8.22 us (7%)
  between operations  6.37 us (5%)
    all_to_all x1, blocking collectives, exchange(): return lax.all_to_all(blocks, axes, 0, 0, tiled=True)  37.5 us
    all_to_all x3, waiting for transfers between devices, exchange(): return lax.all_to_all(blocks, axes, 0, 0, tiled=True)  26.4 us
    all_to_all x3, starting transfers between devices, exchange(): return lax.all_to_all(blocks, axes, 0, 0, tiled=True)  13.5 us
    unnamed x20, local copies, waits for them, and re-layouts  7.09 us
    dot_general x1, matrix products, body(): lax.dot_general(row_half, col_half, (((1,), (1,)), ((), ())), preferred_e...  6.91 us
    ppermute x2, starting transfers between devices, swap(): return lax.ppermute(block, 'core', [(0, 1), (1, 0)])  3.97 us
  transfers between devices with their start and end apart: 5, of which 4 were waited for; matrix products, arithmetic and copies ran while one was open for 11% of the time, Pallas kernels for 0%

profile of v1, /device:TPU:8, one launch (start us, length us, event | category | flops | bytes accessed | tf_op | source)
XLA Modules:
  0.0 118.3 jit_solution(10687802154846360878)
XLA Ops:
  0.6 1.3 %reduce_sum.40 = s32[]{:T(128)} reduce(s32[768]{0:T(1024)} %param.10, s32[]{:T(128)} %constant.37.clone.1), dimensions={0}, to_apply=%region_1.0 | reduce | flops 767 | bytes 3080 | tf_op jit(solution)/shard_map/reduce_sum | solution.py:48
  6.2 0.6 compare_reduce_fusion
  7.4 0.8 convert_bitcast_fusion.1
  8.1 1.4 %broadcast_select_fusion.1 = bf16[1,3]{1,0:T(2,128)(2,1)S(1)} fusion(pred[]{:T(512)} %compare_reduce_fusion, bf16[1,1]{1,0:T(2,128)(2,1)} %bitcast.3, bf16[1,1]{1,0:T(2,128)(2,1)} %bitcast.2, bf16[1,1]{1,0:T(2,128)(2,1)} %bitcast.1), kind=kLoop, calls=%fused_computation.33 | loop fusion | flops 21 | bytes 13 | tf_op jit(solution)/shard_map/select.7
  9.5 0.1 broadcast_in_dim.4
  9.6 37.5 %all_to_all.20 = bf16[32,19,300]{2,1,0:T(8,128)(2,1)S(1)} all-to-all(bf16[32,19,300]{2,1,0:T(8,128)(2,1)S(1)} %broadcast_in_dim.4), channel_id=1, replica_groups=mesh['zh'=4,'y'=8,'core'=2,'x'=4,'zl'=2] {'zh','y'}, dimensions={0} | all-to-all | bytes 729600 | tf_op jit(solution)/shard_map/all_to_all | solution.py:32
  47.1 0.1 copy.37
  47.2 1.9 %collective-permute-start = (bf16[32,19,300]{2,0,1:T(8,128)(2,1)S(1)}, bf16[32,19,300]{2,0,1:T(8,128)(2,1)S(1)}, u32[]{:S(2)}, u32[]{:S(2)}) collective-permute-start(bf16[32,19,300]{2,0,1:T(8,128)(2,1)S(1)} %copy.37), channel_id=1, source_target_pairs={{0,8},{8,0},{1,9},{9,1},{2,10},{10,2},{3,11},{11,3},{4,12},{12,4},... | collective-permute-start | bytes 1094408 | tf_op jit(solution)/shard_map/ppermute | solution.py:36
  49.1 0.9 convert_bitcast_fusion
  50.0 0.9 broadcast_in_dim.5
  50.9 5.2 %all-to-all-start.1 = ((bf16[8,96,300]{2,1,0:T(8,128)(2,1)}), bf16[8,96,300]{2,1,0:T(8,128)(2,1)S(1)}, u32[]{:S(2)}, u32[]{:S(2)}) async-start(bf16[8,96,300]{2,1,0:T(8,128)(2,1)} %broadcast_in_dim.5), calls=%async_computation.1 | async-start | bytes 1179648 | tf_op jit(solution)/shard_map/all_to_all | solution.py:32
  56.1 5.2 %copy.35 = s32[768,1152]{0,1:T(8,128)} copy(s32[768,1152]{1,0:T(8,128)} %param.9) | data formatting | bytes 7077888 | tf_op args[0]
  61.3 0.0 copy-done.6
  61.3 0.0 collective-permute-done
  61.3 0.2 select_bitcast_fusion.1
  61.5 0.0 copy-start.5
  61.5 0.3 slice_maximum_fusion
  61.8 0.1 copy.40
  61.9 1.4 %reshape.97 = bf16[1152,300]{1,0:T(8,128)(2,1)} reshape(bf16[32,2,18,300]{3,2,1,0:T(8,128)(2,1)S(1)} %copy.40) | data formatting | bytes 1382400 | tf_op jit(solution)/shard_map/reshape | solution.py:59
  63.4 0.7 fusion.8
  64.7 2.8 %all-to-all-done.1 = bf16[8,96,300]{2,1,0:T(8,128)(2,1)S(1)} async-done(((bf16[8,96,300]{2,1,0:T(8,128)(2,1)}), bf16[8,96,300]{2,1,0:T(8,128)(2,1)S(1)}, u32[]{:S(2)}, u32[]{:S(2)}) %all-to-all-start.1) | async-done | bytes 460832 | tf_op jit(solution)/shard_map/all_to_all | solution.py:32
  67.6 6.9 %select_convert_fusion = bf16[768,1152]{0,1:T(8,128)(2,1)S(1)} fusion(bf16[1152,300]{1,0:T(8,128)(2,1)} %reshape.97, bf16[768,300]{1,0:T(8,128)(2,1)S(1)} %bitcast.47, s32[768,1152]{0,1:T(8,128)} %copy.35, f32[1152]{0:T(1024)S(1)} %convert_log_fusion, f32[768]{0:T(1024)S(1)} %log_subtract_fusion), kind=kOutput, calls=%fused_computation.2 | convolution fusion | flops 543227904 | bytes 6468096 | tf_op jit(solution)/shard_map/dot_general | solution.py:62
  74.5 0.8 convolution_convert_fusion
  75.3 0.8 convolution_convert_fusion.1
  76.2 0.9 copy.45
  77.0 0.3 reshape.100
  77.4 1.1 copy.50
  78.4 3.7 %all-to-all-start.2 = ((bf16[8,96,300]{2,1,0:T(8,128)(2,1)}), bf16[8,96,300]{2,1,0:T(8,128)(2,1)S(1)}, u32[]{:S(2)}, u32[]{:S(2)}) async-start(bf16[8,96,300]{2,1,0:T(8,128)(2,1)} %bitcast.9), calls=%async_computation.2 | async-start | bytes 1179648 | tf_op jit(solution)/shard_map/all_to_all | solution.py:32
  82.1 0.0 copy-start.2
  82.1 0.1 broadcast_select_fusion
  82.2 0.1 copy.56
  82.3 0.0 copy-start.3
  82.3 0.0 copy-start.4
  82.3 2.1 %collective-permute-start.1 = (bf16[32,18,300]{2,0,1:T(8,128)(2,1)S(1)}, bf16[32,18,300]{2,0,1:T(8,128)(2,1)S(1)}, u32[]{:S(2)}, u32[]{:S(2)}) collective-permute-start(bf16[32,18,300]{2,0,1:T(8,128)(2,1)S(1)} %bitcast.49), channel_id=1, source_target_pairs={{0,8},{8,0},{1,9},{9,1},{2,10},{10,2},{3,11},{11,3},{4,12},{12,4},... | collective-permute-start | bytes 1036808 | tf_op jit(solution)/shard_map/ppermute | solution.py:36
  84.3 1.8 %collective-permute-done.1 = bf16[32,18,300]{2,0,1:T(8,128)(2,1)S(1)} collective-permute-done((bf16[32,18,300]{2,0,1:T(8,128)(2,1)S(1)}, bf16[32,18,300]{2,0,1:T(8,128)(2,1)S(1)}, u32[]{:S(2)}, u32[]{:S(2)}) %collective-permute-start.1) | collective-permute-done | bytes 345632 | tf_op jit(solution)/shard_map/ppermute | solution.py:36
  86.1 1.1 fusion.1
  87.2 5.5 %all-to-all-done.2 = bf16[8,96,300]{2,1,0:T(8,128)(2,1)S(1)} async-done(((bf16[8,96,300]{2,1,0:T(8,128)(2,1)}), bf16[8,96,300]{2,1,0:T(8,128)(2,1)S(1)}, u32[]{:S(2)}, u32[]{:S(2)}) %all-to-all-start.2) | async-done | bytes 460832 | tf_op jit(solution)/shard_map/all_to_all | solution.py:32
  92.7 4.7 %all-to-all-start.3 = ((bf16[32,18,300]{2,1,0:T(8,128)(2,1)}), bf16[32,18,300]{2,1,0:T(8,128)(2,1)S(1)}, u32[]{:S(2)}, u32[]{:S(2)}) async-start(bf16[32,18,300]{2,1,0:T(8,128)(2,1)} %fusion.1), calls=%async_computation.3 | async-start | bytes 1179648 | tf_op jit(solution)/shard_map/all_to_all | solution.py:32
  97.4 0.1 copy.44
  97.5 0.1 copy.43
  97.6 0.1 convert_reduce_fusion.1
  97.7 0.1 copy.51
  97.9 0.8 copy.48
  98.6 0.8 copy.49
  99.4 18.1 %all-to-all-done.3 = bf16[32,18,300]{2,1,0:T(8,128)(2,1)S(1)} async-done(((bf16[32,18,300]{2,1,0:T(8,128)(2,1)}), bf16[32,18,300]{2,1,0:T(8,128)(2,1)S(1)}, u32[]{:S(2)}, u32[]{:S(2)}) %all-to-all-start.3) | async-done | bytes 345632 | tf_op jit(solution)/shard_map/all_to_all | solution.py:32
  117.5 0.1 convert_reduce_fusion
  117.6 0.0 copy-done.3
  117.6 0.6 fusion.5
  (12 shorter events, 0.1 us)
Async XLA Ops:
  47.2 14.1 %collective-permute-start = (bf16[32,19,300]{2,0,1:T(8,128)(2,1)S(1)}, bf16[32,19,300]{2,0,1:T(8,128)(2,1)S(1)}, u32[]{:S(2)}, u32[]{:S(2)}) collective-permute-start(bf16[32,19,300]{2,0,1:T(8,128)(2,1)S(1)} %copy.37), channel_id=1, source_target_pairs={{0,8},{8,0},{1,9},{9,1},{2,10},{10,2},{3,11},{11,3},{4,12},{12,4},... | collective-permute-start | bytes 1094408 | tf_op jit(solution)/shard_map/ppermute | solution.py:36
  50.9 16.7 %all-to-all-start.1 = ((bf16[8,96,300]{2,1,0:T(8,128)(2,1)}), bf16[8,96,300]{2,1,0:T(8,128)(2,1)S(1)}, u32[]{:S(2)}, u32[]{:S(2)}) async-start(bf16[8,96,300]{2,1,0:T(8,128)(2,1)} %broadcast_in_dim.5), calls=%async_computation.1 | async-start | bytes 1179648 | tf_op jit(solution)/shard_map/all_to_all | solution.py:32
  56.1 5.2 %copy-start.6 = (s32[1152]{0:T(1024)S(1)}, s32[1152]{0:T(1024)}, u32[]{:S(2)}) copy-start(s32[1152]{0:T(1024)} %param.11) | copy-start | bytes 13828
  61.5 3.2 %copy-start.5 = (s32[768]{0:T(1024)S(1)}, s32[768]{0:T(1024)}, u32[]{:S(2)}) copy-start(s32[768]{0:T(1024)} %param.10) | copy-start | bytes 9220
  67.6 7.8 %copy-start = (bf16[1152,300]{1,0:T(8,128)(2,1)S(1)}, bf16[1152,300]{1,0:T(8,128)(2,1)}, u32[]{:S(2)}) copy-start(bf16[1152,300]{1,0:T(8,128)(2,1)} %reshape.97) | copy-start | bytes 2073604
  78.4 18.9 %copy-start.1 = (f32[300,96]{0,1:T(8,128)S(1)}, f32[300,96]{0,1:T(8,128)}, u32[]{:S(2)}) copy-start(f32[300,96]{0,1:T(8,128)} %param.12) | copy-start | bytes 345604
  78.4 14.2 %all-to-all-start.2 = ((bf16[8,96,300]{2,1,0:T(8,128)(2,1)}), bf16[8,96,300]{2,1,0:T(8,128)(2,1)S(1)}, u32[]{:S(2)}, u32[]{:S(2)}) async-start(bf16[8,96,300]{2,1,0:T(8,128)(2,1)} %bitcast.9), calls=%async_computation.2 | async-start | bytes 1179648 | tf_op jit(solution)/shard_map/all_to_all | solution.py:32
  82.1 15.4 %copy-start.2 = (f32[300,96]{0,1:T(8,128)S(1)}, f32[300,96]{0,1:T(8,128)}, u32[]{:S(2)}) copy-start(f32[300,96]{0,1:T(8,128)} %param.14) | copy-start | bytes 345604
  82.3 35.4 %copy-start.3 = (f32[300,18]{0,1:T(8,128)S(1)}, f32[300,18]{0,1:T(8,128)}, u32[]{:S(2)}) copy-start(f32[300,18]{0,1:T(8,128)} %param.13) | copy-start | bytes 64804
  82.3 35.3 %copy-start.4 = (f32[300,18]{0,1:T(8,128)S(1)}, f32[300,18]{0,1:T(8,128)}, u32[]{:S(2)}) copy-start(f32[300,18]{0,1:T(8,128)} %param.15) | copy-start | bytes 64804
  82.3 3.8 %collective-permute-start.1 = (bf16[32,18,300]{2,0,1:T(8,128)(2,1)S(1)}, bf16[32,18,300]{2,0,1:T(8,128)(2,1)S(1)}, u32[]{:S(2)}, u32[]{:S(2)}) collective-permute-start(bf16[32,18,300]{2,0,1:T(8,128)(2,1)S(1)} %bitcast.49), channel_id=1, source_target_pairs={{0,8},{8,0},{1,9},{9,1},{2,10},{10,2},{3,11},{11,3},{4,12},{12,4},... | collective-permute-start | bytes 1036808 | tf_op jit(solution)/shard_map/ppermute | solution.py:36
  92.7 24.8 %all-to-all-start.3 = ((bf16[32,18,300]{2,1,0:T(8,128)(2,1)}), bf16[32,18,300]{2,1,0:T(8,128)(2,1)S(1)}, u32[]{:S(2)}, u32[]{:S(2)}) async-start(bf16[32,18,300]{2,1,0:T(8,128)(2,1)} %fusion.1), calls=%async_computation.3 | async-start | bytes 1179648 | tf_op jit(solution)/shard_map/all_to_all | solution.py:32

commit v2 on v1

v2 whole, which is shorter than its diff:
```python
import functools

import jax
import jax.numpy as jnp
from jax import lax
from jax.experimental import pallas as pl
from jax.experimental.pallas import tpu as pltpu
from jax.sharding import Mesh, PartitionSpec as P

ROW_AXES = ("zh", "y", "core")
COL_AXES = ("x", "zl")
CHIP_AXES = ("zh", "y")
GROUP = 24
WINDOW = 640
WIDE = 384
F32, BF16 = jnp.float32, jnp.bfloat16
PARAMS = pltpu.CompilerParams(vmem_limit_bytes=20 * 1024 * 1024)


def widen(value):
    rows, depth = value.shape
    return jnp.concatenate([value, jnp.zeros((rows, WIDE - depth), value.dtype)], axis=1)


def prep_kernel(marg_hbm, col_hbm, row_hbm, send_ref, own_ref, marg, block, rows, sems):
    words = col_hbm.shape[0]
    load_marg = pltpu.make_async_copy(marg_hbm, marg, sems.at[0])
    load_col = pltpu.make_async_copy(col_hbm, block, sems.at[1])
    load_row = pltpu.make_async_copy(row_hbm, rows, sems.at[2])
    load_marg.start()
    load_col.start()
    load_row.start()
    load_marg.wait()
    total = jnp.sum(marg[...], axis=(0, 1), keepdims=True).astype(F32)
    high = total.astype(BF16).astype(F32)
    middle = (total - high).astype(BF16).astype(F32)
    low = total - high - middle
    line = lax.broadcasted_iota(jnp.int32, (GROUP - words, WIDE), 0)
    lane = lax.broadcasted_iota(jnp.int32, (GROUP - words, WIDE), 1)
    parts = jnp.where(lane == 0, high, jnp.where(lane == 1, middle, jnp.where(lane == 2, low, 0.0)))
    load_col.wait()
    value = jnp.concatenate([widen(block[...]), jnp.where(line == 0, parts, 0.0)], axis=0).astype(BF16)
    for i in range(send_ref.shape[0]):
        send_ref[i] = value
    load_row.wait()
    own_ref[...] = widen(rows[...]).astype(BF16)


def prepare(row_marg, col_t, row_t, n_chip):
    return pl.pallas_call(
        prep_kernel,
        in_specs=[pl.BlockSpec(memory_space=pltpu.HBM)] * 3,
        out_shape=(
            jax.ShapeDtypeStruct((n_chip, GROUP, WIDE), BF16),
            jax.ShapeDtypeStruct((row_t.shape[0], WIDE), BF16),
        ),
        scratch_shapes=[
            pltpu.VMEM(row_marg.shape, jnp.int32),
            pltpu.VMEM(col_t.shape, F32),
            pltpu.VMEM(row_t.shape, F32),
            pltpu.SemaphoreType.DMA((3,)),
        ],
        compiler_params=PARAMS,
    )(*[pltpu.with_memory_space_constraint(a, pltpu.HBM) for a in (row_marg, col_t, row_t)])


def group_of(number):
    return jnp.right_shift(number * 2731, 16)


def cells_kernel(words, marg_ref, counts_hbm, count_ref, logs_ref, counts, pick, sems):
    rows, cols = counts_hbm.shape
    cells = count_ref.shape[0] // 2
    half = cells // 2
    block = 256
    loads = [
        pltpu.make_async_copy(counts_hbm.at[r : r + block], counts.at[r : r + block], sems.at[r // block])
        for r in range(0, rows, block)
    ]
    for load in loads:
        load.start()
    log = jnp.log(marg_ref[...].astype(F32))
    high = log.astype(BF16).astype(F32)
    middle = (log - high).astype(BF16).astype(F32)
    low = log - high - middle
    line = lax.broadcasted_iota(jnp.int32, (128, cols), 0)
    stack = jnp.where(line == 0, high, jnp.where(line == 1, middle, jnp.where(line == 2, low, 1.0)))
    stack = stack.astype(BF16)
    lane = lax.broadcasted_iota(jnp.int32, (half, WINDOW), 1)
    place = lax.broadcasted_iota(jnp.int32, (half, 1), 0)
    group = group_of(place)
    word = place - GROUP * group
    column = lax.broadcasted_iota(jnp.int32, (half, 128), 1)
    for m in range(2):
        window = slice(m * (cols - WINDOW), m * (cols - WINDOW) + WINDOW)
        for c in range(2):
            target = (2 * group + (m * half // GROUP * 2 + c)) * words + word - window.start
            target = jnp.where(word < words, target, -1)
            at = slice(c * cells + m * half, c * cells + (m + 1) * half)
            hit = jnp.where(lane == target, 1.0, 0.0).astype(BF16)
            pick[at, :] = hit
            found = lax.dot_general(hit, stack[:, window], (((1,), (1,)), ((), ())), preferred_element_type=F32)
            found = jnp.where(column < 3, found, 0.0)
            found = jnp.where((column == 0) & (word >= words), -1e30, found)
            logs_ref[at, :] = found.astype(BF16)
    for r in range(0, rows, block):
        loads[r // block].wait()
        for m in range(2):
            window = slice(m * (cols - WINDOW), m * (cols - WINDOW) + WINDOW)
            part = counts[r : r + block, window].astype(F32).astype(BF16)
            for c in range(2):
                at = slice(c * cells + m * half, c * cells + (m + 1) * half)
                count = lax.dot_general(pick[at, :], part, (((1,), (1,)), ((), ())), preferred_element_type=F32)
                count_ref[at, r : r + block] = count.astype(jnp.int32).astype(jnp.int8)


def cell_tables(counts, col_marg, n_chip, words):
    rows, cols = counts.shape
    cells = n_chip * GROUP
    return pl.pallas_call(
        functools.partial(cells_kernel, words),
        in_specs=[pl.BlockSpec(memory_space=pltpu.VMEM), pl.BlockSpec(memory_space=pltpu.HBM)],
        out_shape=(jax.ShapeDtypeStruct((2 * cells, rows), jnp.int8), jax.ShapeDtypeStruct((2 * cells, 128), BF16)),
        scratch_shapes=[
            pltpu.VMEM((rows, cols), jnp.int32),
            pltpu.VMEM((2 * cells, WINDOW), BF16),
            pltpu.SemaphoreType.DMA((rows // 256,)),
        ],
        compiler_params=PARAMS,
    )(col_marg, pltpu.with_memory_space_constraint(counts, pltpu.HBM))


def rows_kernel(place_ref, mine_ref, other_ref, out_ref):
    x, zl = place_ref[0], place_ref[1]
    for i in range(4):
        block = 2 * jnp.bitwise_xor(x, i) + zl
        out_ref[block] = mine_ref[i]
        out_ref[jnp.bitwise_xor(block, 1)] = other_ref[i]


def assemble_rows(place, mine, other):
    n, size, depth = mine.shape
    return pl.pallas_call(
        rows_kernel,
        grid_spec=pltpu.PrefetchScalarGridSpec(
            num_scalar_prefetch=1,
            grid=(1,),
            in_specs=[pl.BlockSpec((n, size, depth), lambda i, s: (0, 0, 0))] * 2,
            out_specs=pl.BlockSpec((2 * n, size, depth), lambda i, s: (0, 0, 0)),
        ),
        out_shape=jax.ShapeDtypeStruct((2 * n, size, depth), BF16),
        compiler_params=PARAMS,
    )(place, mine, other)


def slope_kernel(words, half_ref, col_ref, rest_ref, row_ref, marg_ref, count_ref, logs_ref, slope_ref, grad_ref):
    cells, rows = slope_ref.shape
    place = lax.broadcasted_iota(jnp.int32, (16, cells), 1)
    pick = jnp.where(place - GROUP * group_of(place) == words, 1.0, 0.0).astype(BF16)
    parts = jnp.dot(pick, col_ref[...], preferred_element_type=F32)
    parts += jnp.dot(pick, rest_ref[...], preferred_element_type=F32)
    log_total = jnp.log(jnp.sum(parts[0:1, 0:128], axis=1, keepdims=True))
    row_base = jnp.log(marg_ref[...].astype(F32)) - log_total
    first = half_ref[0] * cells
    row_half = row_ref[...]
    block = 256
    for b in range(0, cells, block):
        at = pl.ds(pl.multiple_of(first + b, block), block)
        score = lax.dot_general(
            col_ref[b : b + block, :], row_half, (((1,), (1,)), ((), ())), preferred_element_type=F32
        )
        count = count_ref[at, :].astype(jnp.int32).astype(F32)
        logs = logs_ref[at, :].astype(F32)
        excess = score + (row_base + (logs[:, 0:1] + logs[:, 1:2] + logs[:, 2:3]))
        fitted = (0.1 + 0.25 * jnp.sqrt(count)) * (excess - jnp.log(jnp.maximum(count, 1.0)))
        slope = jnp.where(count > 0.0, fitted, 0.5 + 0.5 * jnp.tanh(0.5 * excess)).astype(BF16)
        slope_ref[b : b + block, :] = slope
        grad = jnp.dot(slope, row_half, preferred_element_type=F32)
        grad_ref[b : b + block, :] = grad.astype(grad_ref.dtype)


def slopes(half, col_half, col_rest, row_half, row_marg, count, logs, words, kind):
    cells, rows = col_half.shape[0], row_half.shape[0]
    vmem = pl.BlockSpec(memory_space=pltpu.VMEM)
    return pl.pallas_call(
        functools.partial(slope_kernel, words),
        in_specs=[pl.BlockSpec(memory_space=pltpu.SMEM)] + [vmem] * 6,
        out_shape=[jax.ShapeDtypeStruct((cells, rows), BF16), jax.ShapeDtypeStruct((cells, WIDE), kind)],
        compiler_params=PARAMS,
    )(half, col_half, col_rest, row_half, row_marg, count, logs)


def row_grad_kernel(place_ref, own_ref, other_ref, keep_slope_ref, give_slope_ref, keep_ref, give_ref, total):
    x, zl = place_ref[0], place_ref[1]
    size = keep_ref.shape[1]
    contract = (((0,), (0,)), ((), ()))
    grad = lax.dot_general(own_ref[...], keep_slope_ref[...], contract, preferred_element_type=F32)
    grad += lax.dot_general(other_ref[...], give_slope_ref[...], contract, preferred_element_type=F32)
    total[...] = grad.T
    for i in range(4):
        block = 2 * jnp.bitwise_xor(x, i) + zl
        keep_ref[i] = total[pl.ds(pl.multiple_of(block * size, size), size), :]
        block = jnp.bitwise_xor(block, 1)
        give_ref[i] = total[pl.ds(pl.multiple_of(block * size, size), size), :].astype(BF16)


def row_grads(place, own, other, keep_slope, give_slope, size):
    rows = keep_slope.shape[1]
    vmem = pl.BlockSpec(memory_space=pltpu.VMEM)
    return pl.pallas_call(
        row_grad_kernel,
        in_specs=[pl.BlockSpec(memory_space=pltpu.SMEM)] + [vmem] * 4,
        out_shape=[
            jax.ShapeDtypeStruct((4, size, WIDE), F32),
            jax.ShapeDtypeStruct((4, size, WIDE), BF16),
        ],
        scratch_shapes=[pltpu.VMEM((rows, WIDE), F32)],
        compiler_params=PARAMS,
    )(place, own, other, keep_slope, give_slope)


def after(value, *others):
    anywhere = pl.BlockSpec(memory_space=pl.ANY)
    return pl.pallas_call(
        lambda *refs: None,
        in_specs=[anywhere] * (1 + len(others)),
        out_specs=anywhere,
        out_shape=jax.ShapeDtypeStruct(value.shape, value.dtype),
        input_output_aliases={0: 0},
        compiler_params=pltpu.CompilerParams(vmem_limit_bytes=1024 * 1024),
    )(value, *others)


def adagrad(embedding, accumulator, gradient):
    new_acc = accumulator + gradient * gradient
    return (embedding - gradient / jnp.sqrt(new_acc), new_acc)


def exchange(blocks):
    return lax.all_to_all(blocks, CHIP_AXES, 0, 0, tiled=True)


def flip(block, axis, mask):
    return lax.ppermute(block, axis, [(i, i ^ mask) for i in range(lax.axis_size(axis))])


def body(counts, row_marg, col_marg, row_emb, col_emb, row_acc, col_acc):
    n_chip = lax.axis_size(CHIP_AXES)
    rows, cols = counts.shape
    depth, words = col_emb.shape
    size = row_emb.shape[1]
    core = lax.axis_index("core")
    place = jnp.stack([lax.axis_index("x"), lax.axis_index("zl"), core]).astype(jnp.int32)

    row_line, col_line = row_marg.reshape(1, rows), col_marg.reshape(1, cols)
    send, own = prepare(row_marg.reshape(rows // 128, 128), col_emb.T, row_emb.T, n_chip)
    mine = exchange(send)
    stack = jnp.stack([own] + [flip(own, "x", k) for k in (1, 2, 3)])
    row_half = assemble_rows(place, stack, flip(stack, "zl", 1)).reshape(rows, WIDE)
    count, logs = cell_tables(counts, col_line, n_chip, words)
    shape = (n_chip, GROUP, WIDE)
    mine = after(mine, row_half, count)
    far = flip(mine, "core", 1).reshape(n_chip * GROUP, WIDE)
    near = mine.reshape(n_chip * GROUP, WIDE)

    give_slope, give = slopes((1 - core).reshape(1), far, near, row_half, row_line, count, logs, words, BF16)
    other = flip(give.reshape(shape), "core", 1)
    keep_slope, keep = slopes(core.reshape(1), near, far, row_half, row_line, count, logs, words, F32)
    pair = (keep.reshape(shape) + other.astype(F32)).astype(BF16)
    col_share = jnp.sum(exchange(pair)[:, :words, :depth].astype(F32), axis=0)

    row_keep, row_give = row_grads(place, near, far, keep_slope, give_slope, size)
    row_keep = row_keep + flip(row_give, "zl", 1).astype(F32)
    row_share = row_keep[0]
    for k in (1, 2, 3):
        row_share = row_share + flip(row_keep[k].astype(BF16), "x", k).astype(F32)
    row_share = row_share[:, :depth]

    new_row_emb, new_row_acc = adagrad(row_emb.T, row_acc.T, row_share)
    new_col_emb, new_col_acc = adagrad(col_emb.T, col_acc.T, col_share)
    return (new_row_emb.T, new_col_emb.T, new_row_acc.T, new_col_acc.T)


def solution(mesh):
    fine = Mesh(mesh.devices.reshape(4, 8, 2, 4, 2), ("zh", "y", "core", "x", "zl"))
    return jax.shard_map(
        body,
        mesh=fine,
        in_specs=(
            P(ROW_AXES, COL_AXES),
            P(ROW_AXES),
            P(COL_AXES),
            P(None, ROW_AXES + COL_AXES),
            P(None, COL_AXES + ROW_AXES),
            P(None, ROW_AXES + COL_AXES),
            P(None, COL_AXES + ROW_AXES),
        ),
        out_specs=(
            P(None, ROW_AXES + COL_AXES),
            P(None, COL_AXES + ROW_AXES),
            P(None, ROW_AXES + COL_AXES),
            P(None, COL_AXES + ROW_AXES),
        ),
        check_vma=False,
    )
```

time: 119 us -> 94.9 us (0.80)
  starting transfers between devices: 17.5 us -> 57.8 us
  blocking collectives: 37.5 us -> 0 us
  Pallas kernels: 0 us -> 13.7 us
  local copies, waits for them, and re-layouts: 11.9 us -> 0.08 us
  waiting for transfers between devices: 28.1 us -> 19 us
  matrix products: 8.59 us -> 0 us
  other arithmetic: 8.22 us -> 2.71 us
  between operations: 6.37 us -> 0.96 us
    all_to_all x1 -> x0, blocking collectives: 37.5 us -> none  [exchange(): return lax.all_to_all(blocks, axes, 0, 0, tiled=True)]
    ppermute x2 -> x10, starting transfers between devices: 3.97 us -> 30.6 us  [flip(): lax.ppermute(block, axis, [(i, i ^ mask) for i in range(lax.axis_size(axi...]
    all_to_all x3 -> x2, waiting for transfers between devices: 26.4 us -> 5.79 us  [exchange(): return lax.all_to_all(blocks, CHIP_AXES, 0, 0, tiled=True)]
    pallas_call x0 -> x7, Pallas kernels: none -> 13.7 us  [the longest x2 5.61 us: slopes(): pl.pallas_call(functools.partial(slope_kernel, words), in_specs=[pl.Block...]
    all_to_all x3 -> x2, starting transfers between devices: 13.5 us -> 27.2 us  [exchange(): return lax.all_to_all(blocks, CHIP_AXES, 0, 0, tiled=True)]
    ppermute x2 -> x10, waiting for transfers between devices: 1.76 us -> 13.2 us  [flip(): lax.ppermute(block, axis, [(i, i ^ mask) for i in range(lax.axis_size(axi...]
    dot_general x3 -> x0, matrix products: 8.59 us -> none  [the longest x1 6.91 us: body(): lax.dot_general(row_half, col_half, (((1,), (1,)), ((), ())), preferred_e...]
    unnamed x20 -> x12, local copies, waits for them, and re-layouts: 7.09 us -> 0.04 us
  transfers between devices with their start and end apart: 5 -> 12, of which waited for: 4 -> 7; matrix products, arithmetic and copies ran while one was open for 11% -> 2% of each run, Pallas kernels for 0% -> 10%
where the time goes in v2:
time: 94.9 us; the launch traced here: 94.3 us
  starting transfers between devices  57.8 us (61%)
  waiting for transfers between devices  19 us (20%)
  Pallas kernels  13.7 us (14%)
  other arithmetic  2.71 us (3%)
  between operations  0.96 us (1%)
    ppermute x10, starting transfers between devices, flip(): lax.ppermute(block, axis, [(i, i ^ mask) for i in range(lax.axis_size(axi...  30.6 us
    all_to_all x2, starting transfers between devices, exchange(): return lax.all_to_all(blocks, CHIP_AXES, 0, 0, tiled=True)  27.2 us
    ppermute x10, waiting for transfers between devices, flip(): lax.ppermute(block, axis, [(i, i ^ mask) for i in range(lax.axis_size(axi...  13.2 us
    all_to_all x2, waiting for transfers between devices, exchange(): return lax.all_to_all(blocks, CHIP_AXES, 0, 0, tiled=True)  5.79 us
    pallas_call x2, Pallas kernels, slopes(): pl.pallas_call(functools.partial(slope_kernel, words), in_specs=[pl.Block...  5.61 us
    pallas_call x1, Pallas kernels, cell_tables(): pl.pallas_call(functools.partial(cells_kernel, words), in_specs=[pl.Block...  3.77 us
    pallas_call x1, Pallas kernels, row_grads(): pl.pallas_call(row_grad_kernel, in_specs=[pl.BlockSpec(memory_space=pltpu...  1.91 us
  transfers between devices with their start and end apart: 12, of which 7 were waited for; matrix products, arithmetic and copies ran while one was open for 2% of the time, Pallas kernels for 10%

profile of v2, /device:TPU:8, one launch (start us, length us, event | category | flops | bytes accessed | tf_op | source)
XLA Modules:
  0.0 94.3 jit_solution(9335434741318821894)
XLA Ops:
  0.6 0.0 copy-start.5
  0.6 1.8 %shard_map.102 = (bf16[32,24,384]{2,1,0:T(8,128)(2,1)}, bf16[96,384]{1,0:T(8,128)(2,1)S(1)}) custom-call(s32[6,128]{1,0:T(8,128)} %bitcast.60, f32[18,300]{1,0:T(8,128)} %bitcast.56, f32[96,300]{1,0:T(8,128)} %bitcast.55), custom_call_target="tpu_custom_call" | custom-call | tf_op jit(solution)/shard_map/pallas_call | solution.py:50
  2.5 16.2 %all-to-all-start = ((bf16[32,24,384]{2,1,0:T(8,128)(2,1)}), bf16[32,24,384]{2,1,0:T(8,128)(2,1)S(1)}, u32[]{:S(2)}, u32[]{:S(2)}) async-start(bf16[32,24,384]{2,1,0:T(8,128)(2,1)} %get-tuple-element.14), calls=%async_computation | async-start | bytes 1179648 | tf_op jit(solution)/shard_map/all_to_all | solution.py:240
  18.7 4.7 %collective-permute-start.2 = (bf16[96,384]{1,0:T(8,128)(2,1)S(1)}, bf16[96,384]{1,0:T(8,128)(2,1)S(1)}, u32[]{:S(2)}, u32[]{:S(2)}) collective-permute-start(bf16[96,384]{1,0:T(8,128)(2,1)S(1)} %get-tuple-element.15), channel_id=1, source_target_pairs={{0,6},{2,4},{4,2},{6,0},{1,7},{3,5},{5,3},{7,1},{8,14},{10,12},{12... | collective-permute-start | bytes 221192 | tf_op jit(solution)/shard_map/ppermute | solution.py:244
  23.3 2.7 %collective-permute-start.1 = (bf16[96,384]{1,0:T(8,128)(2,1)S(1)}, bf16[96,384]{1,0:T(8,128)(2,1)S(1)}, u32[]{:S(2)}, u32[]{:S(2)}) collective-permute-start(bf16[96,384]{1,0:T(8,128)(2,1)S(1)} %get-tuple-element.15), channel_id=1, source_target_pairs={{0,4},{2,6},{4,0},{6,2},{1,5},{3,7},{5,1},{7,3},{8,12},{10,14},{12... | collective-permute-start | bytes 221192 | tf_op jit(solution)/shard_map/ppermute | solution.py:244
  26.1 2.4 %collective-permute-start = (bf16[96,384]{1,0:T(8,128)(2,1)S(1)}, bf16[96,384]{1,0:T(8,128)(2,1)S(1)}, u32[]{:S(2)}, u32[]{:S(2)}) collective-permute-start(bf16[96,384]{1,0:T(8,128)(2,1)S(1)} %get-tuple-element.15), channel_id=1, source_target_pairs={{0,2},{2,0},{4,6},{6,4},{1,3},{3,1},{5,7},{7,5},{8,10},{10,8},{12,... | collective-permute-start | bytes 221192 | tf_op jit(solution)/shard_map/ppermute | solution.py:244
  28.5 0.0 collective-permute-done.2
  28.5 2.9 %collective-permute-done.1 = bf16[96,384]{1,0:T(8,128)(2,1)S(1)} collective-permute-done((bf16[96,384]{1,0:T(8,128)(2,1)S(1)}, bf16[96,384]{1,0:T(8,128)(2,1)S(1)}, u32[]{:S(2)}, u32[]{:S(2)}) %collective-permute-start.1) | collective-permute-done | bytes 73760 | tf_op jit(solution)/shard_map/ppermute | solution.py:244
  31.5 0.8 collective-permute-done
  32.4 3.4 %collective-permute-start.3 = (bf16[4,96,384]{2,1,0:T(8,128)(2,1)S(1)}, bf16[4,96,384]{2,1,0:T(8,128)(2,1)S(1)}, u32[]{:S(2)}, u32[]{:S(2)}) collective-permute-start(bf16[4,96,384]{2,1,0:T(8,128)(2,1)S(1)} %pad_maximum_fusion.mine_ref), channel_id=1, source_target_pairs={{0,1},{1,0},{2,3},{3,2},{4,5},{5,4},{6,7},{7,6},{8,9},{9,8},{10,11... | collective-permute-start | bytes 884744 | tf_op jit(solution)/shard_map/ppermute | solution.py:244
  35.8 0.0 copy-done.5
  35.8 3.8 %shard_map.104 = (s8[1536,768]{1,0:T(32,128)(4,1)S(1)}, bf16[1536,128]{1,0:T(8,128)(2,1)S(1)}) custom-call(s32[1,1152]{1,0:T(1,128)S(1)} %reshape.41.marg_ref, s32[768,1152]{1,0:T(8,128)} %counts_hbm.1), custom_call_target="tpu_custom_call" | custom-call | tf_op jit(solution)/shard_map/pallas_call | solution.py:120
  39.6 0.1 pad_add_fusion.place_ref
  39.6 2.5 %collective-permute-done.3.other_ref = bf16[4,96,384]{2,1,0:T(8,128)(2,1)S(1)} collective-permute-done((bf16[4,96,384]{2,1,0:T(8,128)(2,1)S(1)}, bf16[4,96,384]{2,1,0:T(8,128)(2,1)S(1)}, u32[]{:S(2)}, u32[]{:S(2)}) %collective-permute-start.3) | collective-permute-done | bytes 294944 | tf_op jit(solution)/shard_map/ppermute | solution.py:244
  42.1 0.6 shard_map.103
  42.7 0.0 all-to-all-done.refs_0_
  42.8 0.0 copy-start.4
  42.8 1.9 %collective-permute-start.4 = (bf16[32,24,384]{2,1,0:T(8,128)(2,1)S(1)}, bf16[32,24,384]{2,1,0:T(8,128)(2,1)S(1)}, u32[]{:S(2)}, u32[]{:S(2)}) collective-permute-start(bf16[32,24,384]{2,1,0:T(8,128)(2,1)S(1)} %shard_map.105), channel_id=1, source_target_pairs={{0,8},{8,0},{1,9},{9,1},{2,10},{10,2},{3,11},{11,3},{4,12},{12,4},... | collective-permute-start | bytes 1769480 | tf_op jit(solution)/shard_map/ppermute | solution.py:244
  44.7 0.0 copy-done.4
  44.7 1.9 %collective-permute-done.4 = bf16[32,24,384]{2,1,0:T(8,128)(2,1)S(1)} collective-permute-done((bf16[32,24,384]{2,1,0:T(8,128)(2,1)S(1)}, bf16[32,24,384]{2,1,0:T(8,128)(2,1)S(1)}, u32[]{:S(2)}, u32[]{:S(2)}) %collective-permute-start.4) | collective-permute-done | bytes 589856 | tf_op jit(solution)/shard_map/ppermute | solution.py:244
  46.7 2.8 %shard_map.107 = (bf16[768,768]{1,0:T(8,128)(2,1)S(1)}, bf16[768,384]{1,0:T(8,128)(2,1)S(1)}) custom-call(s32[1]{0:T(128)} %bitcast.13.half_ref, bf16[768,384]{1,0:T(8,128)(2,1)S(1)} %bitcast.49, bf16[768,384]{1,0:T(8,128)(2,1)S(1)} %bitcast.43, bf16[768,384]{1,0:T(8,128)(2,1)S(1)} %bitcast.47, s32[1,768]{1,0:T(1,128)S(1)} %reshape.44.marg_ref, ...), custom_call_target="tpu_custom_call" | custom-call | tf_op jit(solution)/shard_map/pallas_call | solution.py:185
  49.5 2.1 %collective-permute-start.9 = (bf16[32,24,384]{2,1,0:T(8,128)(2,1)S(1)}, bf16[32,24,384]{2,1,0:T(8,128)(2,1)S(1)}, u32[]{:S(2)}, u32[]{:S(2)}) collective-permute-start(bf16[32,24,384]{2,1,0:T(8,128)(2,1)S(1)} %bitcast.54), channel_id=1, source_target_pairs={{0,8},{8,0},{1,9},{9,1},{2,10},{10,2},{3,11},{11,3},{4,12},{12,4},... | collective-permute-start | bytes 1769480 | tf_op jit(solution)/shard_map/ppermute | solution.py:244
  51.5 2.8 %shard_map.106 = (bf16[768,768]{1,0:T(8,128)(2,1)S(1)}, f32[768,384]{1,0:T(8,128)S(1)}) custom-call(s32[1]{0:T(128)} %bitcast.3.half_ref, bf16[768,384]{1,0:T(8,128)(2,1)S(1)} %bitcast.44, bf16[768,384]{1,0:T(8,128)(2,1)S(1)} %bitcast.50, bf16[768,384]{1,0:T(8,128)(2,1)S(1)} %bitcast.48, s32[1,768]{1,0:T(1,128)S(1)} %reshape.44.marg_ref, ...), custom_call_target="tpu_custom_call" | custom-call | tf_op jit(solution)/shard_map/pallas_call | solution.py:185
  54.4 1.9 %shard_map.108 = (f32[4,96,384]{2,1,0:T(8,128)S(1)}, bf16[4,96,384]{2,1,0:T(8,128)(2,1)S(1)}) custom-call(s32[3]{0:T(128)S(1)} %pad_add_fusion.place_ref, bf16[768,384]{1,0:T(8,128)(2,1)S(1)} %bitcast.45, bf16[768,384]{1,0:T(8,128)(2,1)S(1)} %bitcast.51, bf16[768,768]{1,0:T(8,128)(2,1)S(1)} %get-tuple-element.18.keep_slope_ref, ...), custom_call_target="tpu_custom_call" | custom-call | tf_op jit(solution)/shard_map/pallas_call | solution.py:210
  56.3 3.5 %collective-permute-start.5 = (bf16[4,96,384]{2,1,0:T(8,128)(2,1)S(1)}, bf16[4,96,384]{2,1,0:T(8,128)(2,1)S(1)}, u32[]{:S(2)}, u32[]{:S(2)}) collective-permute-start(bf16[4,96,384]{2,1,0:T(8,128)(2,1)S(1)} %get-tuple-element.21), channel_id=1, source_target_pairs={{0,1},{1,0},{2,3},{3,2},{4,5},{5,4},{6,7},{7,6},{8,9},{9,8},{10,11... | collective-permute-start | bytes 884744 | tf_op jit(solution)/shard_map/ppermute | solution.py:244
  59.7 0.0 collective-permute-done.9
  59.8 1.0 %add_convert_fusion = bf16[32,24,384]{2,1,0:T(8,128)(2,1)} fusion(f32[32,24,384]{2,1,0:T(8,128)S(1)} %bitcast.52, bf16[32,24,384]{2,1,0:T(8,128)(2,1)S(1)} %collective-permute-done.9), kind=kLoop, calls=%fused_computation.1 | loop fusion | flops 884736 | bytes 2359296 | tf_op jit(solution)/shard_map/convert_element_type | solution.py:269
  60.7 11.0 %all-to-all-start.1 = ((bf16[32,24,384]{2,1,0:T(8,128)(2,1)}), bf16[32,24,384]{2,1,0:T(8,128)(2,1)S(1)}, u32[]{:S(2)}, u32[]{:S(2)}) async-start(bf16[32,24,384]{2,1,0:T(8,128)(2,1)} %add_convert_fusion), calls=%async_computation.1 | async-start | bytes 1179648 | tf_op jit(solution)/shard_map/all_to_all | solution.py:240
  71.8 0.0 collective-permute-done.5
  71.8 0.0 copy-start
  71.8 0.0 copy-start.2
  71.8 0.1 fusion.6
  71.9 0.0 copy-start.1
  71.9 0.0 copy-start.3
  71.9 3.2 %collective-permute-start.6 = (bf16[96,384]{1,0:T(8,128)(2,1)S(1)}, bf16[96,384]{1,0:T(8,128)(2,1)S(1)}, u32[]{:S(2)}, u32[]{:S(2)}) collective-permute-start(bf16[96,384]{1,0:T(8,128)(2,1)S(1)} %get-tuple-element.30), channel_id=1, source_target_pairs={{0,2},{2,0},{4,6},{6,4},{1,3},{3,1},{5,7},{7,5},{8,10},{10,8},{12,... | collective-permute-start | bytes 221192 | tf_op jit(solution)/shard_map/ppermute | solution.py:244
  75.1 4.1 %collective-permute-start.8 = (bf16[96,384]{1,0:T(8,128)(2,1)S(1)}, bf16[96,384]{1,0:T(8,128)(2,1)S(1)}, u32[]{:S(2)}, u32[]{:S(2)}) collective-permute-start(bf16[96,384]{1,0:T(8,128)(2,1)S(1)} %get-tuple-element.31), channel_id=1, source_target_pairs={{0,6},{2,4},{4,2},{6,0},{1,7},{3,5},{5,3},{7,1},{8,14},{10,12},{12... | collective-permute-start | bytes 221192 | tf_op jit(solution)/shard_map/ppermute | solution.py:244
  79.2 2.7 %collective-permute-start.7 = (bf16[96,384]{1,0:T(8,128)(2,1)S(1)}, bf16[96,384]{1,0:T(8,128)(2,1)S(1)}, u32[]{:S(2)}, u32[]{:S(2)}) collective-permute-start(bf16[96,384]{1,0:T(8,128)(2,1)S(1)} %get-tuple-element.32), channel_id=1, source_target_pairs={{0,4},{2,6},{4,0},{6,2},{1,5},{3,7},{5,1},{7,3},{8,12},{10,14},{12... | collective-permute-start | bytes 221192 | tf_op jit(solution)/shard_map/ppermute | solution.py:244
  81.9 0.0 collective-permute-done.6
  81.9 0.6 collective-permute-done.8
  82.6 4.4 %collective-permute-done.7 = bf16[96,384]{1,0:T(8,128)(2,1)S(1)} collective-permute-done((bf16[96,384]{1,0:T(8,128)(2,1)S(1)}, bf16[96,384]{1,0:T(8,128)(2,1)S(1)}, u32[]{:S(2)}, u32[]{:S(2)}) %collective-permute-start.7) | collective-permute-done | bytes 73760 | tf_op jit(solution)/shard_map/ppermute | solution.py:244
  86.9 0.0 copy-done
  86.9 0.0 copy-done.2
  86.9 0.8 fusion.2
  87.7 5.8 %all-to-all-done.1 = bf16[32,24,384]{2,1,0:T(8,128)(2,1)S(1)} async-done(((bf16[32,24,384]{2,1,0:T(8,128)(2,1)}), bf16[32,24,384]{2,1,0:T(8,128)(2,1)S(1)}, u32[]{:S(2)}, u32[]{:S(2)}) %all-to-all-start.1) | async-done | bytes 589856 | tf_op jit(solution)/shard_map/all_to_all | solution.py:240
  93.5 0.1 convert_reduce_fusion
  93.6 0.0 copy-done.1
  93.6 0.0 copy-done.3
  93.6 0.6 fusion.4
  (6 shorter events, 0.1 us)
Async XLA Ops:
  0.6 35.1 %copy-start.5 = (s32[1152]{0:T(1024)S(1)}, s32[1152]{0:T(1024)}, u32[]{:S(2)}) copy-start(s32[1152]{0:T(1024)} %param.9) | copy-start | bytes 13828
  2.5 40.3 %all-to-all-start = ((bf16[32,24,384]{2,1,0:T(8,128)(2,1)}), bf16[32,24,384]{2,1,0:T(8,128)(2,1)S(1)}, u32[]{:S(2)}, u32[]{:S(2)}) async-start(bf16[32,24,384]{2,1,0:T(8,128)(2,1)} %get-tuple-element.14), calls=%async_computation | async-start | bytes 1179648 | tf_op jit(solution)/shard_map/all_to_all | solution.py:240
  18.7 9.8 %collective-permute-start.2 = (bf16[96,384]{1,0:T(8,128)(2,1)S(1)}, bf16[96,384]{1,0:T(8,128)(2,1)S(1)}, u32[]{:S(2)}, u32[]{:S(2)}) collective-permute-start(bf16[96,384]{1,0:T(8,128)(2,1)S(1)} %get-tuple-element.15), channel_id=1, source_target_pairs={{0,6},{2,4},{4,2},{6,0},{1,7},{3,5},{5,3},{7,1},{8,14},{10,12},{12... | collective-permute-start | bytes 221192 | tf_op jit(solution)/shard_map/ppermute | solution.py:244
  23.3 8.1 %collective-permute-start.1 = (bf16[96,384]{1,0:T(8,128)(2,1)S(1)}, bf16[96,384]{1,0:T(8,128)(2,1)S(1)}, u32[]{:S(2)}, u32[]{:S(2)}) collective-permute-start(bf16[96,384]{1,0:T(8,128)(2,1)S(1)} %get-tuple-element.15), channel_id=1, source_target_pairs={{0,4},{2,6},{4,0},{6,2},{1,5},{3,7},{5,1},{7,3},{8,12},{10,14},{12... | collective-permute-start | bytes 221192 | tf_op jit(solution)/shard_map/ppermute | solution.py:244
  26.1 6.2 %collective-permute-start = (bf16[96,384]{1,0:T(8,128)(2,1)S(1)}, bf16[96,384]{1,0:T(8,128)(2,1)S(1)}, u32[]{:S(2)}, u32[]{:S(2)}) collective-permute-start(bf16[96,384]{1,0:T(8,128)(2,1)S(1)} %get-tuple-element.15), channel_id=1, source_target_pairs={{0,2},{2,0},{4,6},{6,4},{1,3},{3,1},{5,7},{7,5},{8,10},{10,8},{12,... | collective-permute-start | bytes 221192 | tf_op jit(solution)/shard_map/ppermute | solution.py:244
  32.4 9.8 %collective-permute-start.3 = (bf16[4,96,384]{2,1,0:T(8,128)(2,1)S(1)}, bf16[4,96,384]{2,1,0:T(8,128)(2,1)S(1)}, u32[]{:S(2)}, u32[]{:S(2)}) collective-permute-start(bf16[4,96,384]{2,1,0:T(8,128)(2,1)S(1)} %pad_maximum_fusion.mine_ref), channel_id=1, source_target_pairs={{0,1},{1,0},{2,3},{3,2},{4,5},{5,4},{6,7},{7,6},{8,9},{9,8},{10,11... | collective-permute-start | bytes 884744 | tf_op jit(solution)/shard_map/ppermute | solution.py:244
  42.8 2.0 %copy-start.4 = (s32[768]{0:T(1024)S(1)}, s32[768]{0:T(1024)}, u32[]{:S(2)}) copy-start(s32[768]{0:T(1024)} %param.8) | copy-start | bytes 9220
  42.8 3.9 %collective-permute-start.4 = (bf16[32,24,384]{2,1,0:T(8,128)(2,1)S(1)}, bf16[32,24,384]{2,1,0:T(8,128)(2,1)S(1)}, u32[]{:S(2)}, u32[]{:S(2)}) collective-permute-start(bf16[32,24,384]{2,1,0:T(8,128)(2,1)S(1)} %shard_map.105), channel_id=1, source_target_pairs={{0,8},{8,0},{1,9},{9,1},{2,10},{10,2},{3,11},{11,3},{4,12},{12,4},... | collective-permute-start | bytes 1769480 | tf_op jit(solution)/shard_map/ppermute | solution.py:244
  49.5 10.3 %collective-permute-start.9 = (bf16[32,24,384]{2,1,0:T(8,128)(2,1)S(1)}, bf16[32,24,384]{2,1,0:T(8,128)(2,1)S(1)}, u32[]{:S(2)}, u32[]{:S(2)}) collective-permute-start(bf16[32,24,384]{2,1,0:T(8,128)(2,1)S(1)} %bitcast.54), channel_id=1, source_target_pairs={{0,8},{8,0},{1,9},{9,1},{2,10},{10,2},{3,11},{11,3},{4,12},{12,4},... | collective-permute-start | bytes 1769480 | tf_op jit(solution)/shard_map/ppermute | solution.py:244
  56.3 15.5 %collective-permute-start.5 = (bf16[4,96,384]{2,1,0:T(8,128)(2,1)S(1)}, bf16[4,96,384]{2,1,0:T(8,128)(2,1)S(1)}, u32[]{:S(2)}, u32[]{:S(2)}) collective-permute-start(bf16[4,96,384]{2,1,0:T(8,128)(2,1)S(1)} %get-tuple-element.21), channel_id=1, source_target_pairs={{0,1},{1,0},{2,3},{3,2},{4,5},{5,4},{6,7},{7,6},{8,9},{9,8},{10,11... | collective-permute-start | bytes 884744 | tf_op jit(solution)/shard_map/ppermute | solution.py:244
  60.7 32.8 %all-to-all-start.1 = ((bf16[32,24,384]{2,1,0:T(8,128)(2,1)}), bf16[32,24,384]{2,1,0:T(8,128)(2,1)S(1)}, u32[]{:S(2)}, u32[]{:S(2)}) async-start(bf16[32,24,384]{2,1,0:T(8,128)(2,1)} %add_convert_fusion), calls=%async_computation.1 | async-start | bytes 1179648 | tf_op jit(solution)/shard_map/all_to_all | solution.py:240
  71.8 15.2 %copy-start = (f32[300,96]{0,1:T(8,128)S(1)}, f32[300,96]{0,1:T(8,128)}, u32[]{:S(2)}) copy-start(f32[300,96]{0,1:T(8,128)} %param.10) | copy-start | bytes 345604
  71.8 15.2 %copy-start.2 = (f32[300,96]{0,1:T(8,128)S(1)}, f32[300,96]{0,1:T(8,128)}, u32[]{:S(2)}) copy-start(f32[300,96]{0,1:T(8,128)} %param.12) | copy-start | bytes 345604
  71.9 21.7 %copy-start.1 = (f32[300,18]{0,1:T(8,128)S(1)}, f32[300,18]{0,1:T(8,128)}, u32[]{:S(2)}) copy-start(f32[300,18]{0,1:T(8,128)} %param.11) | copy-start | bytes 64804
  71.9 21.7 %copy-start.3 = (f32[300,18]{0,1:T(8,128)S(1)}, f32[300,18]{0,1:T(8,128)}, u32[]{:S(2)}) copy-start(f32[300,18]{0,1:T(8,128)} %param.13) | copy-start | bytes 64804
  71.9 10.0 %collective-permute-start.6 = (bf16[96,384]{1,0:T(8,128)(2,1)S(1)}, bf16[96,384]{1,0:T(8,128)(2,1)S(1)}, u32[]{:S(2)}, u32[]{:S(2)}) collective-permute-start(bf16[96,384]{1,0:T(8,128)(2,1)S(1)} %get-tuple-element.30), channel_id=1, source_target_pairs={{0,2},{2,0},{4,6},{6,4},{1,3},{3,1},{5,7},{7,5},{8,10},{10,8},{12,... | collective-permute-start | bytes 221192 | tf_op jit(solution)/shard_map/ppermute | solution.py:244
  75.1 7.5 %collective-permute-start.8 = (bf16[96,384]{1,0:T(8,128)(2,1)S(1)}, bf16[96,384]{1,0:T(8,128)(2,1)S(1)}, u32[]{:S(2)}, u32[]{:S(2)}) collective-permute-start(bf16[96,384]{1,0:T(8,128)(2,1)S(1)} %get-tuple-element.31), channel_id=1, source_target_pairs={{0,6},{2,4},{4,2},{6,0},{1,7},{3,5},{5,3},{7,1},{8,14},{10,12},{12... | collective-permute-start | bytes 221192 | tf_op jit(solution)/shard_map/ppermute | solution.py:244
  79.2 7.8 %collective-permute-start.7 = (bf16[96,384]{1,0:T(8,128)(2,1)S(1)}, bf16[96,384]{1,0:T(8,128)(2,1)S(1)}, u32[]{:S(2)}, u32[]{:S(2)}) collective-permute-start(bf16[96,384]{1,0:T(8,128)(2,1)S(1)} %get-tuple-element.32), channel_id=1, source_target_pairs={{0,4},{2,6},{4,0},{6,2},{1,5},{3,7},{5,1},{7,3},{8,12},{10,14},{12... | collective-permute-start | bytes 221192 | tf_op jit(solution)/shard_map/ppermute | solution.py:244

commit v3 on v2

--- a/solution.py
+++ b/solution.py
@@ -22,46 +22,61 @@
     return jnp.concatenate([value, jnp.zeros((rows, WIDE - depth), value.dtype)], axis=1)
 
 
-def prep_kernel(marg_hbm, col_hbm, row_hbm, send_ref, own_ref, marg, block, rows, sems):
-    words = col_hbm.shape[0]
+def own_kernel(marg_hbm, row_hbm, col_hbm, own_ref, col_ref, total_ref, marg, rows, cols, sems):
     load_marg = pltpu.make_async_copy(marg_hbm, marg, sems.at[0])
-    load_col = pltpu.make_async_copy(col_hbm, block, sems.at[1])
-    load_row = pltpu.make_async_copy(row_hbm, rows, sems.at[2])
+    load_row = pltpu.make_async_copy(row_hbm, rows, sems.at[1])
+    load_col = pltpu.make_async_copy(col_hbm, cols, sems.at[2])
     load_marg.start()
+    load_row.start()
     load_col.start()
-    load_row.start()
     load_marg.wait()
     total = jnp.sum(marg[...], axis=(0, 1), keepdims=True).astype(F32)
+    total_ref[...] = jnp.broadcast_to(total, total_ref.shape)
+    load_row.wait()
+    own_ref[...] = widen(rows[...]).astype(BF16)
+    load_col.wait()
+    rest = GROUP - cols.shape[0]
+    col_ref[...] = jnp.concatenate([widen(cols[...]), jnp.zeros((rest, WIDE), F32)], axis=0)
+
+
+def prepare_own(row_marg, row_t, col_t):
+    return pl.pallas_call(
+        own_kernel,
+        in_specs=[pl.BlockSpec(memory_space=pltpu.HBM)] * 3,
+        out_shape=(
+            jax.ShapeDtypeStruct((row_t.shape[0], WIDE), BF16),
+            jax.ShapeDtypeStruct((GROUP, WIDE), F32),
+            jax.ShapeDtypeStruct((8, 128), F32),
+        ),
+        scratch_shapes=[
+            pltpu.VMEM(row_marg.shape, jnp.int32),
+            pltpu.VMEM(row_t.shape, F32),
+            pltpu.VMEM(col_t.shape, F32),
+            pltpu.SemaphoreType.DMA((3,)),
+        ],
+        compiler_params=PARAMS,
+    )(*[pltpu.with_memory_space_constraint(a, pltpu.HBM) for a in (row_marg, row_t, col_t)])
+
+
+def send_kernel(words, total_ref, rest_ref, col_ref, send_ref):
+    total = total_ref[0:1, 0:1] + rest_ref[0:1, 0:1]
     high = total.astype(BF16).astype(F32)
     middle = (total - high).astype(BF16).astype(F32)
     low = total - high - middle
-    line = lax.broadcasted_iota(jnp.int32, (GROUP - words, WIDE), 0)
-    lane = lax.broadcasted_iota(jnp.int32, (GROUP - words, WIDE), 1)
+    line = lax.broadcasted_iota(jnp.int32, (GROUP, WIDE), 0)
+    lane = lax.broadcasted_iota(jnp.int32, (GROUP, WIDE), 1)
     parts = jnp.where(lane == 0, high, jnp.where(lane == 1, middle, jnp.where(lane == 2, low, 0.0)))
-    load_col.wait()
-    value = jnp.concatenate([widen(block[...]), jnp.where(line == 0, parts, 0.0)], axis=0).astype(BF16)
+    value = jnp.where(line == words, parts, col_ref[...]).astype(BF16)
     for i in range(send_ref.shape[0]):
         send_ref[i] = value
-    load_row.wait()
-    own_ref[...] = widen(rows[...]).astype(BF16)
-
-
-def prepare(row_marg, col_t, row_t, n_chip):
-    return pl.pallas_call(
-        prep_kernel,
-        in_specs=[pl.BlockSpec(memory_space=pltpu.HBM)] * 3,
-        out_shape=(
-            jax.ShapeDtypeStruct((n_chip, GROUP, WIDE), BF16),
-            jax.ShapeDtypeStruct((row_t.shape[0], WIDE), BF16),
-        ),
-        scratch_shapes=[
-            pltpu.VMEM(row_marg.shape, jnp.int32),
-            pltpu.VMEM(col_t.shape, F32),
-            pltpu.VMEM(row_t.shape, F32),
-            pltpu.SemaphoreType.DMA((3,)),
-        ],
-        compiler_params=PARAMS,
-    )(*[pltpu.with_memory_space_constraint(a, pltpu.HBM) for a in (row_marg, col_t, row_t)])
+
+
+def prepare_send(total, rest, col_own, n_chip, words):
+    return pl.pallas_call(
+        functools.partial(send_kernel, words),
+        out_shape=jax.ShapeDtypeStruct((n_chip, GROUP, WIDE), BF16),
+        compiler_params=PARAMS,
+    )(total, rest, col_own)
 
 
 def group_of(number):
@@ -130,35 +145,30 @@
     )(col_marg, pltpu.with_memory_space_constraint(counts, pltpu.HBM))
 
 
-def rows_kernel(place_ref, mine_ref, other_ref, out_ref):
+def rows_kernel(place_ref, *refs):
     x, zl = place_ref[0], place_ref[1]
-    for i in range(4):
-        block = 2 * jnp.bitwise_xor(x, i) + zl
-        out_ref[block] = mine_ref[i]
-        out_ref[jnp.bitwise_xor(block, 1)] = other_ref[i]
-
-
-def assemble_rows(place, mine, other):
-    n, size, depth = mine.shape
+    for k in range(4):
+        for b in range(2):
+            block = 2 * jnp.bitwise_xor(x, k) + jnp.bitwise_xor(zl, b)
+            refs[4][block] = refs[k][b]
+
+
+def assemble_rows(place, pairs):
+    size, depth = pairs[0].shape[1:]
+    vmem = pl.BlockSpec(memory_space=pltpu.VMEM)
     return pl.pallas_call(
         rows_kernel,
-        grid_spec=pltpu.PrefetchScalarGridSpec(
-            num_scalar_prefetch=1,
-            grid=(1,),
-            in_specs=[pl.BlockSpec((n, size, depth), lambda i, s: (0, 0, 0))] * 2,
-            out_specs=pl.BlockSpec((2 * n, size, depth), lambda i, s: (0, 0, 0)),
-        ),
-        out_shape=jax.ShapeDtypeStruct((2 * n, size, depth), BF16),
-        compiler_params=PARAMS,
-    )(place, mine, other)
-
-
-def slope_kernel(words, half_ref, col_ref, rest_ref, row_ref, marg_ref, count_ref, logs_ref, slope_ref, grad_ref):
+        in_specs=[pl.BlockSpec(memory_space=pltpu.SMEM)] + [vmem] * 4,
+        out_shape=jax.ShapeDtypeStruct((8, size, depth), BF16),
+        compiler_params=PARAMS,
+    )(place, *pairs)
+
+
+def slope_kernel(words, half_ref, order_ref, col_ref, near_ref, row_ref, marg_ref, count_ref, logs_ref, slope_ref, grad_ref):
     cells, rows = slope_ref.shape
     place = lax.broadcasted_iota(jnp.int32, (16, cells), 1)
     pick = jnp.where(place - GROUP * group_of(place) == words, 1.0, 0.0).astype(BF16)
-    parts = jnp.dot(pick, col_ref[...], preferred_element_type=F32)
-    parts += jnp.dot(pick, rest_ref[...], preferred_element_type=F32)
+    parts = jnp.dot(pick, near_ref[...], preferred_element_type=F32)
     log_total = jnp.log(jnp.sum(parts[0:1, 0:128], axis=1, keepdims=True))
     row_base = jnp.log(marg_ref[...].astype(F32)) - log_total
     first = half_ref[0] * cells
@@ -179,15 +189,15 @@
         grad_ref[b : b + block, :] = grad.astype(grad_ref.dtype)
 
 
-def slopes(half, col_half, col_rest, row_half, row_marg, count, logs, words, kind):
+def slopes(half, order, col_half, near, row_half, row_marg, count, logs, words, kind):
     cells, rows = col_half.shape[0], row_half.shape[0]
     vmem = pl.BlockSpec(memory_space=pltpu.VMEM)
     return pl.pallas_call(
         functools.partial(slope_kernel, words),
-        in_specs=[pl.BlockSpec(memory_space=pltpu.SMEM)] + [vmem] * 6,
+        in_specs=[pl.BlockSpec(memory_space=pltpu.SMEM), pl.BlockSpec(memory_space=pl.ANY)] + [vmem] * 6,
         out_shape=[jax.ShapeDtypeStruct((cells, rows), BF16), jax.ShapeDtypeStruct((cells, WIDE), kind)],
         compiler_params=PARAMS,
-    )(half, col_half, col_rest, row_half, row_marg, count, logs)
+    )(half, order, col_half, near, row_half, row_marg, count, logs)
 
 
 def row_grad_kernel(place_ref, own_ref, other_ref, keep_slope_ref, give_slope_ref, keep_ref, give_ref, total):
@@ -253,19 +263,22 @@
     place = jnp.stack([lax.axis_index("x"), lax.axis_index("zl"), core]).astype(jnp.int32)
 
     row_line, col_line = row_marg.reshape(1, rows), col_marg.reshape(1, cols)
-    send, own = prepare(row_marg.reshape(rows // 128, 128), col_emb.T, row_emb.T, n_chip)
-    mine = exchange(send)
-    stack = jnp.stack([own] + [flip(own, "x", k) for k in (1, 2, 3)])
-    row_half = assemble_rows(place, stack, flip(stack, "zl", 1)).reshape(rows, WIDE)
+    own, col_own, total = prepare_own(row_marg.reshape(rows // 128, 128), row_emb.T, col_emb.T)
+    beside = flip(own, "zl", 1)
+    send = prepare_send(total, flip(total, "core", 1), col_own, n_chip, words)
+    mine = exchange(after(send, beside))
+    both = jnp.stack([own, beside])
+    row_half = assemble_rows(place, [both] + [flip(both, "x", k) for k in (1, 2, 3)]).reshape(rows, WIDE)
     count, logs = cell_tables(counts, col_line, n_chip, words)
     shape = (n_chip, GROUP, WIDE)
     mine = after(mine, row_half, count)
     far = flip(mine, "core", 1).reshape(n_chip * GROUP, WIDE)
     near = mine.reshape(n_chip * GROUP, WIDE)
 
-    give_slope, give = slopes((1 - core).reshape(1), far, near, row_half, row_line, count, logs, words, BF16)
+    tables = (near, row_half, row_line, count, logs, words)
+    keep_slope, keep = slopes(core.reshape(1), near, near, *tables, F32)
+    give_slope, give = slopes((1 - core).reshape(1), keep_slope, far, *tables, BF16)
     other = flip(give.reshape(shape), "core", 1)
-    keep_slope, keep = slopes(core.reshape(1), near, far, row_half, row_line, count, logs, words, F32)
     pair = (keep.reshape(shape) + other.astype(F32)).astype(BF16)
     col_share = jnp.sum(exchange(pair)[:, :words, :depth].astype(F32), axis=0)
 

time: 94.9 us -> 90.7 us (0.956)
  starting transfers between devices: 57.8 us -> 54.1 us
    all_to_all x2, starting transfers between devices: 27.2 us -> 20.7 us  [exchange(): return lax.all_to_all(blocks, CHIP_AXES, 0, 0, tiled=True)]
    ppermute x10 -> x11, waiting for transfers between devices: 13.2 us -> 9.41 us  [flip(): lax.ppermute(block, axis, [(i, i ^ mask) for i in range(lax.axis_size(axi...]
    all_to_all x2, waiting for transfers between devices: 5.79 us -> 9.18 us  [exchange(): return lax.all_to_all(blocks, CHIP_AXES, 0, 0, tiled=True)]
    ppermute x10 -> x11, starting transfers between devices: 30.6 us -> 33.4 us  [flip(): lax.ppermute(block, axis, [(i, i ^ mask) for i in range(lax.axis_size(axi...]
    pallas_call x2 -> x3, Pallas kernels: 2.43 us -> 2.51 us  [the longest x1 0.97 us: prepare_own(): pl.pallas_call(own_kernel, in_specs=[pl.BlockSpec(memory_space=pltpu.HBM)...]
  transfers between devices with their start and end apart: 12 -> 13, of which waited for: 7 -> 8; matrix products, arithmetic and copies ran while one was open for 2% -> 2% of each run, Pallas kernels for 10% -> 11%
where the time goes in v3:
time: 90.7 us; the launch traced here: 90 us
  starting transfers between devices  54.1 us (60%)
  waiting for transfers between devices  18.6 us (21%)
  Pallas kernels  13.6 us (15%)
  other arithmetic  2.69 us (3%)
  between operations  0.91 us (1%)
    ppermute x11, starting transfers between devices, flip(): lax.ppermute(block, axis, [(i, i ^ mask) for i in range(lax.axis_size(axi...  33.4 us
    all_to_all x2, starting transfers between devices, exchange(): return lax.all_to_all(blocks, CHIP_AXES, 0, 0, tiled=True)  20.7 us
    ppermute x11, waiting for transfers between devices, flip(): lax.ppermute(block, axis, [(i, i ^ mask) for i in range(lax.axis_size(axi...  9.41 us
    all_to_all x2, waiting for transfers between devices, exchange(): return lax.all_to_all(blocks, CHIP_AXES, 0, 0, tiled=True)  9.18 us
    pallas_call x2, Pallas kernels, slopes(): pl.pallas_call(functools.partial(slope_kernel, words), in_specs=[pl.Block...  5.41 us
    pallas_call x1, Pallas kernels, cell_tables(): pl.pallas_call(functools.partial(cells_kernel, words), in_specs=[pl.Block...  3.77 us
    pallas_call x1, Pallas kernels, row_grads(): pl.pallas_call(row_grad_kernel, in_specs=[pl.BlockSpec(memory_space=pltpu...  1.91 us
  transfers between devices with their start and end apart: 13, of which 8 were waited for; matrix products, arithmetic and copies ran while one was open for 2% of the time, Pallas kernels for 11%

profile of v3, /device:TPU:8, one launch (start us, length us, event | category | flops | bytes accessed | tf_op | source)
XLA Modules:
  0.0 90.0 jit_solution(1611169523797517981)
XLA Ops:
  0.6 1.0 %shard_map.102 = (bf16[96,384]{1,0:T(8,128)(2,1)S(1)}, f32[24,384]{1,0:T(8,128)S(1)}, f32[8,128]{1,0:T(8,128)S(1)}) custom-call(s32[6,128]{1,0:T(8,128)} %bitcast.57, f32[96,300]{1,0:T(8,128)} %bitcast.55, f32[18,300]{1,0:T(8,128)} %bitcast.56), custom_call_target="tpu_custom_call" | custom-call | tf_op jit(solution)/shard_map/pallas_call | solution.py:43
  1.6 4.3 %collective-permute-start.1 = (bf16[96,384]{1,0:T(8,128)(2,1)S(1)}, bf16[96,384]{1,0:T(8,128)(2,1)S(1)}, u32[]{:S(2)}, u32[]{:S(2)}) collective-permute-start(bf16[96,384]{1,0:T(8,128)(2,1)S(1)} %get-tuple-element.17), channel_id=1, source_target_pairs={{0,1},{1,0},{2,3},{3,2},{4,5},{5,4},{6,7},{7,6},{8,9},{9,8},{10,11... | collective-permute-start | bytes 221192 | tf_op jit(solution)/shard_map/ppermute | solution.py:254
  5.9 1.9 %collective-permute-start = (f32[8,128]{1,0:T(8,128)S(1)}, f32[8,128]{1,0:T(8,128)S(1)}, u32[]{:S(2)}, u32[]{:S(2)}) collective-permute-start(f32[8,128]{1,0:T(8,128)S(1)} %get-tuple-element.15.total_ref), channel_id=1, source_target_pairs={{0,8},{8,0},{1,9},{9,1},{2,10},{10,2},{3,11},{11,3},{4,12},{12,4},... | collective-permute-start | bytes 12296 | tf_op jit(solution)/shard_map/ppermute | solution.py:254
  7.8 1.1 %collective-permute-done.rest_ref = f32[8,128]{1,0:T(8,128)S(1)} collective-permute-done((f32[8,128]{1,0:T(8,128)S(1)}, f32[8,128]{1,0:T(8,128)S(1)}, u32[]{:S(2)}, u32[]{:S(2)}) %collective-permute-start) | collective-permute-done | bytes 4128 | tf_op jit(solution)/shard_map/ppermute | solution.py:254
  9.0 0.9 %shard_map.103.refs_0_ = bf16[32,24,384]{2,1,0:T(8,128)(2,1)} custom-call(f32[8,128]{1,0:T(8,128)S(1)} %get-tuple-element.15.total_ref, f32[8,128]{1,0:T(8,128)S(1)} %collective-permute-done.rest_ref, f32[24,384]{1,0:T(8,128)S(1)} %get-tuple-element.16.col_ref), custom_call_target="tpu_custom_call" | custom-call | tf_op jit(solution)/shard_map/pallas_call | solution.py:75
  9.9 0.0 copy-start.5
  9.9 0.0 collective-permute-done.1.refs_1_
  9.9 15.4 %all-to-all-start = ((bf16[32,24,384]{2,1,0:T(8,128)(2,1)}), bf16[32,24,384]{2,1,0:T(8,128)(2,1)S(1)}, u32[]{:S(2)}, u32[]{:S(2)}) async-start(bf16[32,24,384]{2,1,0:T(8,128)(2,1)} %shard_map.104), calls=%async_computation | async-start | bytes 1179648 | tf_op jit(solution)/shard_map/all_to_all | solution.py:250
  25.3 4.7 %collective-permute-start.4 = (bf16[2,96,384]{2,1,0:T(8,128)(2,1)S(1)}, bf16[2,96,384]{2,1,0:T(8,128)(2,1)S(1)}, u32[]{:S(2)}, u32[]{:S(2)}) collective-permute-start(bf16[2,96,384]{2,1,0:T(8,128)(2,1)S(1)} %pad_maximum_fusion.refs_0_), channel_id=1, source_target_pairs={{0,6},{2,4},{4,2},{6,0},{1,7},{3,5},{5,3},{7,1},{8,14},{10,12},{12... | collective-permute-start | bytes 442376 | tf_op jit(solution)/shard_map/ppermute | solution.py:254
  30.0 2.7 %collective-permute-start.3 = (bf16[2,96,384]{2,1,0:T(8,128)(2,1)S(1)}, bf16[2,96,384]{2,1,0:T(8,128)(2,1)S(1)}, u32[]{:S(2)}, u32[]{:S(2)}) collective-permute-start(bf16[2,96,384]{2,1,0:T(8,128)(2,1)S(1)} %pad_maximum_fusion.refs_0_), channel_id=1, source_target_pairs={{0,4},{2,6},{4,0},{6,2},{1,5},{3,7},{5,1},{7,3},{8,12},{10,14},{12... | collective-permute-start | bytes 442376 | tf_op jit(solution)/shard_map/ppermute | solution.py:254
  32.7 2.4 %collective-permute-start.2 = (bf16[2,96,384]{2,1,0:T(8,128)(2,1)S(1)}, bf16[2,96,384]{2,1,0:T(8,128)(2,1)S(1)}, u32[]{:S(2)}, u32[]{:S(2)}) collective-permute-start(bf16[2,96,384]{2,1,0:T(8,128)(2,1)S(1)} %pad_maximum_fusion.refs_0_), channel_id=1, source_target_pairs={{0,2},{2,0},{4,6},{6,4},{1,3},{3,1},{5,7},{7,5},{8,10},{10,8},{12,... | collective-permute-start | bytes 442376 | tf_op jit(solution)/shard_map/ppermute | solution.py:254
  35.2 0.0 copy-done.5
  35.2 3.8 %shard_map.106 = (s8[1536,768]{1,0:T(32,128)(4,1)S(1)}, bf16[1536,128]{1,0:T(8,128)(2,1)S(1)}) custom-call(s32[1,1152]{1,0:T(1,128)S(1)} %reshape.41.marg_ref, s32[768,1152]{1,0:T(8,128)} %counts_hbm.1), custom_call_target="tpu_custom_call" | custom-call | tf_op jit(solution)/shard_map/pallas_call | solution.py:135
  39.0 0.1 pad_add_fusion.place_ref
  39.1 0.0 collective-permute-done.4.refs_3_
  39.1 0.3 collective-permute-done.3.refs_2_
  39.3 0.4 collective-permute-done.2.refs_1_
  39.8 0.6 shard_map.105
  40.4 6.8 %all-to-all-done.refs_0_ = bf16[32,24,384]{2,1,0:T(8,128)(2,1)S(1)} async-done(((bf16[32,24,384]{2,1,0:T(8,128)(2,1)}), bf16[32,24,384]{2,1,0:T(8,128)(2,1)S(1)}, u32[]{:S(2)}, u32[]{:S(2)}) %all-to-all-start) | async-done | bytes 589856 | tf_op jit(solution)/shard_map/all_to_all | solution.py:250
  47.2 2.0 %collective-permute-start.5 = (bf16[32,24,384]{2,1,0:T(8,128)(2,1)S(1)}, bf16[32,24,384]{2,1,0:T(8,128)(2,1)S(1)}, u32[]{:S(2)}, u32[]{:S(2)}) collective-permute-start(bf16[32,24,384]{2,1,0:T(8,128)(2,1)S(1)} %shard_map.107), channel_id=1, source_target_pairs={{0,8},{8,0},{1,9},{9,1},{2,10},{10,2},{3,11},{11,3},{4,12},{12,4},... | collective-permute-start | bytes 1769480 | tf_op jit(solution)/shard_map/ppermute | solution.py:254
  49.2 0.0 copy-done.4
  49.2 2.7 %shard_map.108 = (bf16[768,768]{1,0:T(8,128)(2,1)S(1)}, f32[768,384]{1,0:T(8,128)S(1)}) custom-call(s32[1]{0:T(128)} %bitcast.3.half_ref, bf16[768,384]{1,0:T(8,128)(2,1)S(1)} %bitcast.41, bf16[768,384]{1,0:T(8,128)(2,1)S(1)} %bitcast.42, bf16[768,384]{1,0:T(8,128)(2,1)S(1)} %bitcast.43, bf16[768,384]{1,0:T(8,128)(2,1)S(1)} %bitcast.47, ...), custom_call_target="tpu_custom_call" | custom-call | tf_op jit(solution)/shard_map/pallas_call | solution.py:195
  52.0 0.0 collective-permute-done.5
  52.0 2.7 %shard_map.109 = (bf16[768,768]{1,0:T(8,128)(2,1)S(1)}, bf16[768,384]{1,0:T(8,128)(2,1)S(1)}) custom-call(s32[1]{0:T(128)} %bitcast.11.half_ref, bf16[768,768]{1,0:T(8,128)(2,1)S(1)} %get-tuple-element.20.order_ref.keep_slope_ref, bf16[768,384]{1,0:T(8,128)(2,1)S(1)} %bitcast.49, bf16[768,384]{1,0:T(8,128)(2,1)S(1)} %bitcast.44, ...), custom_call_target="tpu_custom_call" | custom-call | tf_op jit(solution)/shard_map/pallas_call | solution.py:195
  54.7 2.4 %collective-permute-start.10 = (bf16[32,24,384]{2,1,0:T(8,128)(2,1)S(1)}, bf16[32,24,384]{2,1,0:T(8,128)(2,1)S(1)}, u32[]{:S(2)}, u32[]{:S(2)}) collective-permute-start(bf16[32,24,384]{2,1,0:T(8,128)(2,1)S(1)} %bitcast.54), channel_id=1, source_target_pairs={{0,8},{8,0},{1,9},{9,1},{2,10},{10,2},{3,11},{11,3},{4,12},{12,4},... | collective-permute-start | bytes 1769480 | tf_op jit(solution)/shard_map/ppermute | solution.py:254
  57.1 1.9 %shard_map.110 = (f32[4,96,384]{2,1,0:T(8,128)S(1)}, bf16[4,96,384]{2,1,0:T(8,128)(2,1)S(1)}) custom-call(s32[3]{0:T(128)S(1)} %pad_add_fusion.place_ref, bf16[768,384]{1,0:T(8,128)(2,1)S(1)} %bitcast.45, bf16[768,384]{1,0:T(8,128)(2,1)S(1)} %bitcast.50, bf16[768,768]{1,0:T(8,128)(2,1)S(1)} %get-tuple-element.20.order_ref.keep_slope_ref, ...), custom_call_target="tpu_custom_call" | custom-call | tf_op jit(solution)/shard_map/pallas_call | solution.py:220
  59.0 2.5 %collective-permute-start.6 = (bf16[4,96,384]{2,1,0:T(8,128)(2,1)S(1)}, bf16[4,96,384]{2,1,0:T(8,128)(2,1)S(1)}, u32[]{:S(2)}, u32[]{:S(2)}) collective-permute-start(bf16[4,96,384]{2,1,0:T(8,128)(2,1)S(1)} %get-tuple-element.23), channel_id=1, source_target_pairs={{0,1},{1,0},{2,3},{3,2},{4,5},{5,4},{6,7},{7,6},{8,9},{9,8},{10,11... | collective-permute-start | bytes 884744 | tf_op jit(solution)/shard_map/ppermute | solution.py:254
  61.5 0.0 collective-permute-done.10
  61.5 1.0 %add_convert_fusion = bf16[32,24,384]{2,1,0:T(8,128)(2,1)} fusion(f32[32,24,384]{2,1,0:T(8,128)S(1)} %bitcast.51, bf16[32,24,384]{2,1,0:T(8,128)(2,1)S(1)} %collective-permute-done.10), kind=kLoop, calls=%fused_computation.1 | loop fusion | flops 884736 | bytes 2359296 | tf_op jit(solution)/shard_map/convert_element_type | solution.py:282
  62.5 5.3 %all-to-all-start.1 = ((bf16[32,24,384]{2,1,0:T(8,128)(2,1)}), bf16[32,24,384]{2,1,0:T(8,128)(2,1)S(1)}, u32[]{:S(2)}, u32[]{:S(2)}) async-start(bf16[32,24,384]{2,1,0:T(8,128)(2,1)} %add_convert_fusion), calls=%async_computation.1 | async-start | bytes 1179648 | tf_op jit(solution)/shard_map/all_to_all | solution.py:250
  67.8 2.4 %collective-permute-done.6 = bf16[4,96,384]{2,1,0:T(8,128)(2,1)S(1)} collective-permute-done((bf16[4,96,384]{2,1,0:T(8,128)(2,1)S(1)}, bf16[4,96,384]{2,1,0:T(8,128)(2,1)S(1)}, u32[]{:S(2)}, u32[]{:S(2)}) %collective-permute-start.6) | collective-permute-done | bytes 294944 | tf_op jit(solution)/shard_map/ppermute | solution.py:254
  70.2 0.1 fusion.6
  70.3 0.0 copy-start.1
  70.3 0.0 copy-start.3
  70.4 3.9 %collective-permute-start.7 = (bf16[96,384]{1,0:T(8,128)(2,1)S(1)}, bf16[96,384]{1,0:T(8,128)(2,1)S(1)}, u32[]{:S(2)}, u32[]{:S(2)}) collective-permute-start(bf16[96,384]{1,0:T(8,128)(2,1)S(1)} %get-tuple-element.32), channel_id=1, source_target_pairs={{0,2},{2,0},{4,6},{6,4},{1,3},{3,1},{5,7},{7,5},{8,10},{10,8},{12,... | collective-permute-start | bytes 221192 | tf_op jit(solution)/shard_map/ppermute | solution.py:254
  74.3 4.0 %collective-permute-start.9 = (bf16[96,384]{1,0:T(8,128)(2,1)S(1)}, bf16[96,384]{1,0:T(8,128)(2,1)S(1)}, u32[]{:S(2)}, u32[]{:S(2)}) collective-permute-start(bf16[96,384]{1,0:T(8,128)(2,1)S(1)} %get-tuple-element.33), channel_id=1, source_target_pairs={{0,6},{2,4},{4,2},{6,0},{1,7},{3,5},{5,3},{7,1},{8,14},{10,12},{12... | collective-permute-start | bytes 221192 | tf_op jit(solution)/shard_map/ppermute | solution.py:254
  78.3 2.6 %collective-permute-start.8 = (bf16[96,384]{1,0:T(8,128)(2,1)S(1)}, bf16[96,384]{1,0:T(8,128)(2,1)S(1)}, u32[]{:S(2)}, u32[]{:S(2)}) collective-permute-start(bf16[96,384]{1,0:T(8,128)(2,1)S(1)} %get-tuple-element.34), channel_id=1, source_target_pairs={{0,4},{2,6},{4,0},{6,2},{1,5},{3,7},{5,1},{7,3},{8,12},{10,14},{12... | collective-permute-start | bytes 221192 | tf_op jit(solution)/shard_map/ppermute | solution.py:254
  80.9 0.0 collective-permute-done.7
  80.9 0.9 collective-permute-done.9
  81.8 4.3 %collective-permute-done.8 = bf16[96,384]{1,0:T(8,128)(2,1)S(1)} collective-permute-done((bf16[96,384]{1,0:T(8,128)(2,1)S(1)}, bf16[96,384]{1,0:T(8,128)(2,1)S(1)}, u32[]{:S(2)}, u32[]{:S(2)}) %collective-permute-start.8) | collective-permute-done | bytes 73760 | tf_op jit(solution)/shard_map/ppermute | solution.py:254
  86.1 0.0 copy-done
  86.1 0.0 copy-done.2
  86.1 0.8 fusion.2
  86.9 2.4 %all-to-all-done.1 = bf16[32,24,384]{2,1,0:T(8,128)(2,1)S(1)} async-done(((bf16[32,24,384]{2,1,0:T(8,128)(2,1)}), bf16[32,24,384]{2,1,0:T(8,128)(2,1)S(1)}, u32[]{:S(2)}, u32[]{:S(2)}) %all-to-all-start.1) | async-done | bytes 589856 | tf_op jit(solution)/shard_map/all_to_all | solution.py:250
  89.2 0.1 convert_reduce_fusion
  89.4 0.0 copy-done.1
  89.4 0.0 copy-done.3
  89.4 0.6 fusion.4
  (10 shorter events, 0.1 us)
Async XLA Ops:
  1.6 8.3 %collective-permute-start.1 = (bf16[96,384]{1,0:T(8,128)(2,1)S(1)}, bf16[96,384]{1,0:T(8,128)(2,1)S(1)}, u32[]{:S(2)}, u32[]{:S(2)}) collective-permute-start(bf16[96,384]{1,0:T(8,128)(2,1)S(1)} %get-tuple-element.17), channel_id=1, source_target_pairs={{0,1},{1,0},{2,3},{3,2},{4,5},{5,4},{6,7},{7,6},{8,9},{9,8},{10,11... | collective-permute-start | bytes 221192 | tf_op jit(solution)/shard_map/ppermute | solution.py:254
  5.9 3.1 %collective-permute-start = (f32[8,128]{1,0:T(8,128)S(1)}, f32[8,128]{1,0:T(8,128)S(1)}, u32[]{:S(2)}, u32[]{:S(2)}) collective-permute-start(f32[8,128]{1,0:T(8,128)S(1)} %get-tuple-element.15.total_ref), channel_id=1, source_target_pairs={{0,8},{8,0},{1,9},{9,1},{2,10},{10,2},{3,11},{11,3},{4,12},{12,4},... | collective-permute-start | bytes 12296 | tf_op jit(solution)/shard_map/ppermute | solution.py:254
  9.9 25.3 %copy-start.5 = (s32[1152]{0:T(1024)S(1)}, s32[1152]{0:T(1024)}, u32[]{:S(2)}) copy-start(s32[1152]{0:T(1024)} %param.9) | copy-start | bytes 13828
  9.9 37.3 %all-to-all-start = ((bf16[32,24,384]{2,1,0:T(8,128)(2,1)}), bf16[32,24,384]{2,1,0:T(8,128)(2,1)S(1)}, u32[]{:S(2)}, u32[]{:S(2)}) async-start(bf16[32,24,384]{2,1,0:T(8,128)(2,1)} %shard_map.104), calls=%async_computation | async-start | bytes 1179648 | tf_op jit(solution)/shard_map/all_to_all | solution.py:250
  25.3 13.7 %collective-permute-start.4 = (bf16[2,96,384]{2,1,0:T(8,128)(2,1)S(1)}, bf16[2,96,384]{2,1,0:T(8,128)(2,1)S(1)}, u32[]{:S(2)}, u32[]{:S(2)}) collective-permute-start(bf16[2,96,384]{2,1,0:T(8,128)(2,1)S(1)} %pad_maximum_fusion.refs_0_), channel_id=1, source_target_pairs={{0,6},{2,4},{4,2},{6,0},{1,7},{3,5},{5,3},{7,1},{8,14},{10,12},{12... | collective-permute-start | bytes 442376 | tf_op jit(solution)/shard_map/ppermute | solution.py:254
  30.0 9.3 %collective-permute-start.3 = (bf16[2,96,384]{2,1,0:T(8,128)(2,1)S(1)}, bf16[2,96,384]{2,1,0:T(8,128)(2,1)S(1)}, u32[]{:S(2)}, u32[]{:S(2)}) collective-permute-start(bf16[2,96,384]{2,1,0:T(8,128)(2,1)S(1)} %pad_maximum_fusion.refs_0_), channel_id=1, source_target_pairs={{0,4},{2,6},{4,0},{6,2},{1,5},{3,7},{5,1},{7,3},{8,12},{10,14},{12... | collective-permute-start | bytes 442376 | tf_op jit(solution)/shard_map/ppermute | solution.py:254
  32.7 7.0 %collective-permute-start.2 = (bf16[2,96,384]{2,1,0:T(8,128)(2,1)S(1)}, bf16[2,96,384]{2,1,0:T(8,128)(2,1)S(1)}, u32[]{:S(2)}, u32[]{:S(2)}) collective-permute-start(bf16[2,96,384]{2,1,0:T(8,128)(2,1)S(1)} %pad_maximum_fusion.refs_0_), channel_id=1, source_target_pairs={{0,2},{2,0},{4,6},{6,4},{1,3},{3,1},{5,7},{7,5},{8,10},{10,8},{12,... | collective-permute-start | bytes 442376 | tf_op jit(solution)/shard_map/ppermute | solution.py:254
  47.2 2.1 %copy-start.4 = (s32[768]{0:T(1024)S(1)}, s32[768]{0:T(1024)}, u32[]{:S(2)}) copy-start(s32[768]{0:T(1024)} %param.8) | copy-start | bytes 9220
  47.2 4.8 %collective-permute-start.5 = (bf16[32,24,384]{2,1,0:T(8,128)(2,1)S(1)}, bf16[32,24,384]{2,1,0:T(8,128)(2,1)S(1)}, u32[]{:S(2)}, u32[]{:S(2)}) collective-permute-start(bf16[32,24,384]{2,1,0:T(8,128)(2,1)S(1)} %shard_map.107), channel_id=1, source_target_pairs={{0,8},{8,0},{1,9},{9,1},{2,10},{10,2},{3,11},{11,3},{4,12},{12,4},... | collective-permute-start | bytes 1769480 | tf_op jit(solution)/shard_map/ppermute | solution.py:254
  54.7 6.8 %collective-permute-start.10 = (bf16[32,24,384]{2,1,0:T(8,128)(2,1)S(1)}, bf16[32,24,384]{2,1,0:T(8,128)(2,1)S(1)}, u32[]{:S(2)}, u32[]{:S(2)}) collective-permute-start(bf16[32,24,384]{2,1,0:T(8,128)(2,1)S(1)} %bitcast.54), channel_id=1, source_target_pairs={{0,8},{8,0},{1,9},{9,1},{2,10},{10,2},{3,11},{11,3},{4,12},{12,4},... | collective-permute-start | bytes 1769480 | tf_op jit(solution)/shard_map/ppermute | solution.py:254
  59.0 11.2 %collective-permute-start.6 = (bf16[4,96,384]{2,1,0:T(8,128)(2,1)S(1)}, bf16[4,96,384]{2,1,0:T(8,128)(2,1)S(1)}, u32[]{:S(2)}, u32[]{:S(2)}) collective-permute-start(bf16[4,96,384]{2,1,0:T(8,128)(2,1)S(1)} %get-tuple-element.23), channel_id=1, source_target_pairs={{0,1},{1,0},{2,3},{3,2},{4,5},{5,4},{6,7},{7,6},{8,9},{9,8},{10,11... | collective-permute-start | bytes 884744 | tf_op jit(solution)/shard_map/ppermute | solution.py:254
  62.5 26.7 %all-to-all-start.1 = ((bf16[32,24,384]{2,1,0:T(8,128)(2,1)}), bf16[32,24,384]{2,1,0:T(8,128)(2,1)S(1)}, u32[]{:S(2)}, u32[]{:S(2)}) async-start(bf16[32,24,384]{2,1,0:T(8,128)(2,1)} %add_convert_fusion), calls=%async_computation.1 | async-start | bytes 1179648 | tf_op jit(solution)/shard_map/all_to_all | solution.py:250
  70.2 15.9 %copy-start = (f32[300,96]{0,1:T(8,128)S(1)}, f32[300,96]{0,1:T(8,128)}, u32[]{:S(2)}) copy-start(f32[300,96]{0,1:T(8,128)} %param.10) | copy-start | bytes 345604
  70.2 15.9 %copy-start.2 = (f32[300,96]{0,1:T(8,128)S(1)}, f32[300,96]{0,1:T(8,128)}, u32[]{:S(2)}) copy-start(f32[300,96]{0,1:T(8,128)} %param.12) | copy-start | bytes 345604
  70.3 19.1 %copy-start.1 = (f32[300,18]{0,1:T(8,128)S(1)}, f32[300,18]{0,1:T(8,128)}, u32[]{:S(2)}) copy-start(f32[300,18]{0,1:T(8,128)} %param.11) | copy-start | bytes 64804
  70.3 19.1 %copy-start.3 = (f32[300,18]{0,1:T(8,128)S(1)}, f32[300,18]{0,1:T(8,128)}, u32[]{:S(2)}) copy-start(f32[300,18]{0,1:T(8,128)} %param.13) | copy-start | bytes 64804
  70.4 10.6 %collective-permute-start.7 = (bf16[96,384]{1,0:T(8,128)(2,1)S(1)}, bf16[96,384]{1,0:T(8,128)(2,1)S(1)}, u32[]{:S(2)}, u32[]{:S(2)}) collective-permute-start(bf16[96,384]{1,0:T(8,128)(2,1)S(1)} %get-tuple-element.32), channel_id=1, source_target_pairs={{0,2},{2,0},{4,6},{6,4},{1,3},{3,1},{5,7},{7,5},{8,10},{10,8},{12,... | collective-permute-start | bytes 221192 | tf_op jit(solution)/shard_map/ppermute | solution.py:254
  74.3 7.5 %collective-permute-start.9 = (bf16[96,384]{1,0:T(8,128)(2,1)S(1)}, bf16[96,384]{1,0:T(8,128)(2,1)S(1)}, u32[]{:S(2)}, u32[]{:S(2)}) collective-permute-start(bf16[96,384]{1,0:T(8,128)(2,1)S(1)} %get-tuple-element.33), channel_id=1, source_target_pairs={{0,6},{2,4},{4,2},{6,0},{1,7},{3,5},{5,3},{7,1},{8,14},{10,12},{12... | collective-permute-start | bytes 221192 | tf_op jit(solution)/shard_map/ppermute | solution.py:254
  78.3 7.8 %collective-permute-start.8 = (bf16[96,384]{1,0:T(8,128)(2,1)S(1)}, bf16[96,384]{1,0:T(8,128)(2,1)S(1)}, u32[]{:S(2)}, u32[]{:S(2)}) collective-permute-start(bf16[96,384]{1,0:T(8,128)(2,1)S(1)} %get-tuple-element.34), channel_id=1, source_target_pairs={{0,4},{2,6},{4,0},{6,2},{1,5},{3,7},{5,1},{7,3},{8,12},{10,14},{12... | collective-permute-start | bytes 221192 | tf_op jit(solution)/shard_map/ppermute | solution.py:254

commit v4 on v3

--- a/solution.py
+++ b/solution.py
@@ -182,7 +182,8 @@
         count = count_ref[at, :].astype(jnp.int32).astype(F32)
         logs = logs_ref[at, :].astype(F32)
         excess = score + (row_base + (logs[:, 0:1] + logs[:, 1:2] + logs[:, 2:3]))
-        fitted = (0.1 + 0.25 * jnp.sqrt(count)) * (excess - jnp.log(jnp.maximum(count, 1.0)))
+        least = jnp.maximum(count, 1.0)
+        fitted = (0.1 + 0.25 * (least * lax.rsqrt(least))) * (excess - jnp.log(least))
         slope = jnp.where(count > 0.0, fitted, 0.5 + 0.5 * jnp.tanh(0.5 * excess)).astype(BF16)
         slope_ref[b : b + block, :] = slope
         grad = jnp.dot(slope, row_half, preferred_element_type=F32)
@@ -204,9 +205,10 @@
     x, zl = place_ref[0], place_ref[1]
     size = keep_ref.shape[1]
     contract = (((0,), (0,)), ((), ()))
-    grad = lax.dot_general(own_ref[...], keep_slope_ref[...], contract, preferred_element_type=F32)
-    grad += lax.dot_general(other_ref[...], give_slope_ref[...], contract, preferred_element_type=F32)
-    total[...] = grad.T
+    used = 304
+    grad = lax.dot_general(own_ref[:, :used], keep_slope_ref[...], contract, preferred_element_type=F32)
+    grad += lax.dot_general(other_ref[:, :used], give_slope_ref[...], contract, preferred_element_type=F32)
+    total[...] = widen(grad.T)
     for i in range(4):
         block = 2 * jnp.bitwise_xor(x, i) + zl
         keep_ref[i] = total[pl.ds(pl.multiple_of(block * size, size), size), :]

time: 90.7 us -> 89.9 us (level)
  no operation moved by 1% of the time
where the time goes in v4:
time: 89.9 us; the launch traced here: 89.2 us
  starting transfers between devices  54.1 us (60%)
  waiting for transfers between devices  18.6 us (21%)
  Pallas kernels  12.8 us (14%)
  other arithmetic  2.69 us (3%)
  between operations  0.91 us (1%)
    ppermute x11, starting transfers between devices, flip(): lax.ppermute(block, axis, [(i, i ^ mask) for i in range(lax.axis_size(axi...  33.4 us
    all_to_all x2, starting transfers between devices, exchange(): return lax.all_to_all(blocks, CHIP_AXES, 0, 0, tiled=True)  20.7 us
    ppermute x11, waiting for transfers between devices, flip(): lax.ppermute(block, axis, [(i, i ^ mask) for i in range(lax.axis_size(axi...  9.41 us
    all_to_all x2, waiting for transfers between devices, exchange(): return lax.all_to_all(blocks, CHIP_AXES, 0, 0, tiled=True)  9.19 us
    pallas_call x2, Pallas kernels, slopes(): pl.pallas_call(functools.partial(slope_kernel, words), in_specs=[pl.Block...  4.77 us
    pallas_call x1, Pallas kernels, cell_tables(): pl.pallas_call(functools.partial(cells_kernel, words), in_specs=[pl.Block...  3.77 us
  transfers between devices with their start and end apart: 13, of which 8 were waited for; matrix products, arithmetic and copies ran while one was open for 2% of the time, Pallas kernels for 11%

profile of v4, /device:TPU:8, one launch (start us, length us, event | category | flops | bytes accessed | tf_op | source)
XLA Modules:
  0.0 89.2 jit_solution(14990390557736487819)
XLA Ops:
  0.6 1.0 %shard_map.102 = (bf16[96,384]{1,0:T(8,128)(2,1)S(1)}, f32[24,384]{1,0:T(8,128)S(1)}, f32[8,128]{1,0:T(8,128)S(1)}) custom-call(s32[6,128]{1,0:T(8,128)} %bitcast.57, f32[96,300]{1,0:T(8,128)} %bitcast.55, f32[18,300]{1,0:T(8,128)} %bitcast.56), custom_call_target="tpu_custom_call" | custom-call | tf_op jit(solution)/shard_map/pallas_call | solution.py:43
  1.6 4.3 %collective-permute-start.1 = (bf16[96,384]{1,0:T(8,128)(2,1)S(1)}, bf16[96,384]{1,0:T(8,128)(2,1)S(1)}, u32[]{:S(2)}, u32[]{:S(2)}) collective-permute-start(bf16[96,384]{1,0:T(8,128)(2,1)S(1)} %get-tuple-element.17), channel_id=1, source_target_pairs={{0,1},{1,0},{2,3},{3,2},{4,5},{5,4},{6,7},{7,6},{8,9},{9,8},{10,11... | collective-permute-start | bytes 221192 | tf_op jit(solution)/shard_map/ppermute | solution.py:256
  5.9 1.9 %collective-permute-start = (f32[8,128]{1,0:T(8,128)S(1)}, f32[8,128]{1,0:T(8,128)S(1)}, u32[]{:S(2)}, u32[]{:S(2)}) collective-permute-start(f32[8,128]{1,0:T(8,128)S(1)} %get-tuple-element.15.total_ref), channel_id=1, source_target_pairs={{0,8},{8,0},{1,9},{9,1},{2,10},{10,2},{3,11},{11,3},{4,12},{12,4},... | collective-permute-start | bytes 12296 | tf_op jit(solution)/shard_map/ppermute | solution.py:256
  7.8 1.1 %collective-permute-done.rest_ref = f32[8,128]{1,0:T(8,128)S(1)} collective-permute-done((f32[8,128]{1,0:T(8,128)S(1)}, f32[8,128]{1,0:T(8,128)S(1)}, u32[]{:S(2)}, u32[]{:S(2)}) %collective-permute-start) | collective-permute-done | bytes 4128 | tf_op jit(solution)/shard_map/ppermute | solution.py:256
  9.0 0.9 %shard_map.103.refs_0_ = bf16[32,24,384]{2,1,0:T(8,128)(2,1)} custom-call(f32[8,128]{1,0:T(8,128)S(1)} %get-tuple-element.15.total_ref, f32[8,128]{1,0:T(8,128)S(1)} %collective-permute-done.rest_ref, f32[24,384]{1,0:T(8,128)S(1)} %get-tuple-element.16.col_ref), custom_call_target="tpu_custom_call" | custom-call | tf_op jit(solution)/shard_map/pallas_call | solution.py:75
  9.9 0.0 copy-start.5
  9.9 0.0 collective-permute-done.1.refs_1_
  9.9 15.4 %all-to-all-start = ((bf16[32,24,384]{2,1,0:T(8,128)(2,1)}), bf16[32,24,384]{2,1,0:T(8,128)(2,1)S(1)}, u32[]{:S(2)}, u32[]{:S(2)}) async-start(bf16[32,24,384]{2,1,0:T(8,128)(2,1)} %shard_map.104), calls=%async_computation | async-start | bytes 1179648 | tf_op jit(solution)/shard_map/all_to_all | solution.py:252
  25.3 4.7 %collective-permute-start.4 = (bf16[2,96,384]{2,1,0:T(8,128)(2,1)S(1)}, bf16[2,96,384]{2,1,0:T(8,128)(2,1)S(1)}, u32[]{:S(2)}, u32[]{:S(2)}) collective-permute-start(bf16[2,96,384]{2,1,0:T(8,128)(2,1)S(1)} %pad_maximum_fusion.refs_0_), channel_id=1, source_target_pairs={{0,6},{2,4},{4,2},{6,0},{1,7},{3,5},{5,3},{7,1},{8,14},{10,12},{12... | collective-permute-start | bytes 442376 | tf_op jit(solution)/shard_map/ppermute | solution.py:256
  30.0 2.7 %collective-permute-start.3 = (bf16[2,96,384]{2,1,0:T(8,128)(2,1)S(1)}, bf16[2,96,384]{2,1,0:T(8,128)(2,1)S(1)}, u32[]{:S(2)}, u32[]{:S(2)}) collective-permute-start(bf16[2,96,384]{2,1,0:T(8,128)(2,1)S(1)} %pad_maximum_fusion.refs_0_), channel_id=1, source_target_pairs={{0,4},{2,6},{4,0},{6,2},{1,5},{3,7},{5,1},{7,3},{8,12},{10,14},{12... | collective-permute-start | bytes 442376 | tf_op jit(solution)/shard_map/ppermute | solution.py:256
  32.7 2.4 %collective-permute-start.2 = (bf16[2,96,384]{2,1,0:T(8,128)(2,1)S(1)}, bf16[2,96,384]{2,1,0:T(8,128)(2,1)S(1)}, u32[]{:S(2)}, u32[]{:S(2)}) collective-permute-start(bf16[2,96,384]{2,1,0:T(8,128)(2,1)S(1)} %pad_maximum_fusion.refs_0_), channel_id=1, source_target_pairs={{0,2},{2,0},{4,6},{6,4},{1,3},{3,1},{5,7},{7,5},{8,10},{10,8},{12,... | collective-permute-start | bytes 442376 | tf_op jit(solution)/shard_map/ppermute | solution.py:256
  35.2 0.0 copy-done.5
  35.2 3.8 %shard_map.106 = (s8[1536,768]{1,0:T(32,128)(4,1)S(1)}, bf16[1536,128]{1,0:T(8,128)(2,1)S(1)}) custom-call(s32[1,1152]{1,0:T(1,128)S(1)} %reshape.41.marg_ref, s32[768,1152]{1,0:T(8,128)} %counts_hbm.1), custom_call_target="tpu_custom_call" | custom-call | tf_op jit(solution)/shard_map/pallas_call | solution.py:135
  39.0 0.1 pad_add_fusion.place_ref
  39.1 0.0 collective-permute-done.4.refs_3_
  39.1 0.3 collective-permute-done.3.refs_2_
  39.3 0.4 collective-permute-done.2.refs_1_
  39.8 0.6 shard_map.105
  40.4 6.8 %all-to-all-done.refs_0_ = bf16[32,24,384]{2,1,0:T(8,128)(2,1)S(1)} async-done(((bf16[32,24,384]{2,1,0:T(8,128)(2,1)}), bf16[32,24,384]{2,1,0:T(8,128)(2,1)S(1)}, u32[]{:S(2)}, u32[]{:S(2)}) %all-to-all-start) | async-done | bytes 589856 | tf_op jit(solution)/shard_map/all_to_all | solution.py:252
  47.2 2.0 %collective-permute-start.5 = (bf16[32,24,384]{2,1,0:T(8,128)(2,1)S(1)}, bf16[32,24,384]{2,1,0:T(8,128)(2,1)S(1)}, u32[]{:S(2)}, u32[]{:S(2)}) collective-permute-start(bf16[32,24,384]{2,1,0:T(8,128)(2,1)S(1)} %shard_map.107), channel_id=1, source_target_pairs={{0,8},{8,0},{1,9},{9,1},{2,10},{10,2},{3,11},{11,3},{4,12},{12,4},... | collective-permute-start | bytes 1769480 | tf_op jit(solution)/shard_map/ppermute | solution.py:256
  49.2 0.0 copy-done.4
  49.2 2.4 %shard_map.108 = (bf16[768,768]{1,0:T(8,128)(2,1)S(1)}, f32[768,384]{1,0:T(8,128)S(1)}) custom-call(s32[1]{0:T(128)} %bitcast.3.half_ref, bf16[768,384]{1,0:T(8,128)(2,1)S(1)} %bitcast.41, bf16[768,384]{1,0:T(8,128)(2,1)S(1)} %bitcast.42, bf16[768,384]{1,0:T(8,128)(2,1)S(1)} %bitcast.43, bf16[768,384]{1,0:T(8,128)(2,1)S(1)} %bitcast.47, ...), custom_call_target="tpu_custom_call" | custom-call | tf_op jit(solution)/shard_map/pallas_call | solution.py:196
  51.6 0.0 collective-permute-done.5
  51.6 2.4 %shard_map.109 = (bf16[768,768]{1,0:T(8,128)(2,1)S(1)}, bf16[768,384]{1,0:T(8,128)(2,1)S(1)}) custom-call(s32[1]{0:T(128)} %bitcast.11.half_ref, bf16[768,768]{1,0:T(8,128)(2,1)S(1)} %get-tuple-element.20.order_ref.keep_slope_ref, bf16[768,384]{1,0:T(8,128)(2,1)S(1)} %bitcast.49, bf16[768,384]{1,0:T(8,128)(2,1)S(1)} %bitcast.44, ...), custom_call_target="tpu_custom_call" | custom-call | tf_op jit(solution)/shard_map/pallas_call | solution.py:196
  54.0 2.4 %collective-permute-start.10 = (bf16[32,24,384]{2,1,0:T(8,128)(2,1)S(1)}, bf16[32,24,384]{2,1,0:T(8,128)(2,1)S(1)}, u32[]{:S(2)}, u32[]{:S(2)}) collective-permute-start(bf16[32,24,384]{2,1,0:T(8,128)(2,1)S(1)} %bitcast.54), channel_id=1, source_target_pairs={{0,8},{8,0},{1,9},{9,1},{2,10},{10,2},{3,11},{11,3},{4,12},{12,4},... | collective-permute-start | bytes 1769480 | tf_op jit(solution)/shard_map/ppermute | solution.py:256
  56.5 1.7 %shard_map.110 = (f32[4,96,384]{2,1,0:T(8,128)S(1)}, bf16[4,96,384]{2,1,0:T(8,128)(2,1)S(1)}) custom-call(s32[3]{0:T(128)S(1)} %pad_add_fusion.place_ref, bf16[768,384]{1,0:T(8,128)(2,1)S(1)} %bitcast.45, bf16[768,384]{1,0:T(8,128)(2,1)S(1)} %bitcast.50, bf16[768,768]{1,0:T(8,128)(2,1)S(1)} %get-tuple-element.20.order_ref.keep_slope_ref, ...), custom_call_target="tpu_custom_call" | custom-call | tf_op jit(solution)/shard_map/pallas_call | solution.py:222
  58.2 2.5 %collective-permute-start.6 = (bf16[4,96,384]{2,1,0:T(8,128)(2,1)S(1)}, bf16[4,96,384]{2,1,0:T(8,128)(2,1)S(1)}, u32[]{:S(2)}, u32[]{:S(2)}) collective-permute-start(bf16[4,96,384]{2,1,0:T(8,128)(2,1)S(1)} %get-tuple-element.23), channel_id=1, source_target_pairs={{0,1},{1,0},{2,3},{3,2},{4,5},{5,4},{6,7},{7,6},{8,9},{9,8},{10,11... | collective-permute-start | bytes 884744 | tf_op jit(solution)/shard_map/ppermute | solution.py:256
  60.7 0.0 collective-permute-done.10
  60.7 1.0 %add_convert_fusion = bf16[32,24,384]{2,1,0:T(8,128)(2,1)} fusion(f32[32,24,384]{2,1,0:T(8,128)S(1)} %bitcast.51, bf16[32,24,384]{2,1,0:T(8,128)(2,1)S(1)} %collective-permute-done.10), kind=kLoop, calls=%fused_computation.1 | loop fusion | flops 884736 | bytes 2359296 | tf_op jit(solution)/shard_map/convert_element_type | solution.py:284
  61.7 5.3 %all-to-all-start.1 = ((bf16[32,24,384]{2,1,0:T(8,128)(2,1)}), bf16[32,24,384]{2,1,0:T(8,128)(2,1)S(1)}, u32[]{:S(2)}, u32[]{:S(2)}) async-start(bf16[32,24,384]{2,1,0:T(8,128)(2,1)} %add_convert_fusion), calls=%async_computation.1 | async-start | bytes 1179648 | tf_op jit(solution)/shard_map/all_to_all | solution.py:252
  67.0 2.4 %collective-permute-done.6 = bf16[4,96,384]{2,1,0:T(8,128)(2,1)S(1)} collective-permute-done((bf16[4,96,384]{2,1,0:T(8,128)(2,1)S(1)}, bf16[4,96,384]{2,1,0:T(8,128)(2,1)S(1)}, u32[]{:S(2)}, u32[]{:S(2)}) %collective-permute-start.6) | collective-permute-done | bytes 294944 | tf_op jit(solution)/shard_map/ppermute | solution.py:256
  69.4 0.1 fusion.6
  69.5 0.0 copy-start.1
  69.5 0.0 copy-start.3
  69.5 3.9 %collective-permute-start.7 = (bf16[96,384]{1,0:T(8,128)(2,1)S(1)}, bf16[96,384]{1,0:T(8,128)(2,1)S(1)}, u32[]{:S(2)}, u32[]{:S(2)}) collective-permute-start(bf16[96,384]{1,0:T(8,128)(2,1)S(1)} %get-tuple-element.32), channel_id=1, source_target_pairs={{0,2},{2,0},{4,6},{6,4},{1,3},{3,1},{5,7},{7,5},{8,10},{10,8},{12,... | collective-permute-start | bytes 221192 | tf_op jit(solution)/shard_map/ppermute | solution.py:256
  73.5 4.0 %collective-permute-start.9 = (bf16[96,384]{1,0:T(8,128)(2,1)S(1)}, bf16[96,384]{1,0:T(8,128)(2,1)S(1)}, u32[]{:S(2)}, u32[]{:S(2)}) collective-permute-start(bf16[96,384]{1,0:T(8,128)(2,1)S(1)} %get-tuple-element.33), channel_id=1, source_target_pairs={{0,6},{2,4},{4,2},{6,0},{1,7},{3,5},{5,3},{7,1},{8,14},{10,12},{12... | collective-permute-start | bytes 221192 | tf_op jit(solution)/shard_map/ppermute | solution.py:256
  77.5 2.6 %collective-permute-start.8 = (bf16[96,384]{1,0:T(8,128)(2,1)S(1)}, bf16[96,384]{1,0:T(8,128)(2,1)S(1)}, u32[]{:S(2)}, u32[]{:S(2)}) collective-permute-start(bf16[96,384]{1,0:T(8,128)(2,1)S(1)} %get-tuple-element.34), channel_id=1, source_target_pairs={{0,4},{2,6},{4,0},{6,2},{1,5},{3,7},{5,1},{7,3},{8,12},{10,14},{12... | collective-permute-start | bytes 221192 | tf_op jit(solution)/shard_map/ppermute | solution.py:256
  80.1 0.0 collective-permute-done.7
  80.1 0.8 collective-permute-done.9
  81.0 4.3 %collective-permute-done.8 = bf16[96,384]{1,0:T(8,128)(2,1)S(1)} collective-permute-done((bf16[96,384]{1,0:T(8,128)(2,1)S(1)}, bf16[96,384]{1,0:T(8,128)(2,1)S(1)}, u32[]{:S(2)}, u32[]{:S(2)}) %collective-permute-start.8) | collective-permute-done | bytes 73760 | tf_op jit(solution)/shard_map/ppermute | solution.py:256
  85.3 0.0 copy-done
  85.3 0.0 copy-done.2
  85.3 0.8 fusion.2
  86.0 2.4 %all-to-all-done.1 = bf16[32,24,384]{2,1,0:T(8,128)(2,1)S(1)} async-done(((bf16[32,24,384]{2,1,0:T(8,128)(2,1)}), bf16[32,24,384]{2,1,0:T(8,128)(2,1)S(1)}, u32[]{:S(2)}, u32[]{:S(2)}) %all-to-all-start.1) | async-done | bytes 589856 | tf_op jit(solution)/shard_map/all_to_all | solution.py:252
  88.4 0.1 convert_reduce_fusion
  88.6 0.0 copy-done.1
  88.6 0.0 copy-done.3
  88.6 0.6 fusion.4
  (10 shorter events, 0.1 us)
Async XLA Ops:
  1.6 8.3 %collective-permute-start.1 = (bf16[96,384]{1,0:T(8,128)(2,1)S(1)}, bf16[96,384]{1,0:T(8,128)(2,1)S(1)}, u32[]{:S(2)}, u32[]{:S(2)}) collective-permute-start(bf16[96,384]{1,0:T(8,128)(2,1)S(1)} %get-tuple-element.17), channel_id=1, source_target_pairs={{0,1},{1,0},{2,3},{3,2},{4,5},{5,4},{6,7},{7,6},{8,9},{9,8},{10,11... | collective-permute-start | bytes 221192 | tf_op jit(solution)/shard_map/ppermute | solution.py:256
  5.9 3.1 %collective-permute-start = (f32[8,128]{1,0:T(8,128)S(1)}, f32[8,128]{1,0:T(8,128)S(1)}, u32[]{:S(2)}, u32[]{:S(2)}) collective-permute-start(f32[8,128]{1,0:T(8,128)S(1)} %get-tuple-element.15.total_ref), channel_id=1, source_target_pairs={{0,8},{8,0},{1,9},{9,1},{2,10},{10,2},{3,11},{11,3},{4,12},{12,4},... | collective-permute-start | bytes 12296 | tf_op jit(solution)/shard_map/ppermute | solution.py:256
  9.9 25.3 %copy-start.5 = (s32[1152]{0:T(1024)S(1)}, s32[1152]{0:T(1024)}, u32[]{:S(2)}) copy-start(s32[1152]{0:T(1024)} %param.9) | copy-start | bytes 13828
  9.9 37.3 %all-to-all-start = ((bf16[32,24,384]{2,1,0:T(8,128)(2,1)}), bf16[32,24,384]{2,1,0:T(8,128)(2,1)S(1)}, u32[]{:S(2)}, u32[]{:S(2)}) async-start(bf16[32,24,384]{2,1,0:T(8,128)(2,1)} %shard_map.104), calls=%async_computation | async-start | bytes 1179648 | tf_op jit(solution)/shard_map/all_to_all | solution.py:252
  25.3 13.7 %collective-permute-start.4 = (bf16[2,96,384]{2,1,0:T(8,128)(2,1)S(1)}, bf16[2,96,384]{2,1,0:T(8,128)(2,1)S(1)}, u32[]{:S(2)}, u32[]{:S(2)}) collective-permute-start(bf16[2,96,384]{2,1,0:T(8,128)(2,1)S(1)} %pad_maximum_fusion.refs_0_), channel_id=1, source_target_pairs={{0,6},{2,4},{4,2},{6,0},{1,7},{3,5},{5,3},{7,1},{8,14},{10,12},{12... | collective-permute-start | bytes 442376 | tf_op jit(solution)/shard_map/ppermute | solution.py:256
  30.0 9.3 %collective-permute-start.3 = (bf16[2,96,384]{2,1,0:T(8,128)(2,1)S(1)}, bf16[2,96,384]{2,1,0:T(8,128)(2,1)S(1)}, u32[]{:S(2)}, u32[]{:S(2)}) collective-permute-start(bf16[2,96,384]{2,1,0:T(8,128)(2,1)S(1)} %pad_maximum_fusion.refs_0_), channel_id=1, source_target_pairs={{0,4},{2,6},{4,0},{6,2},{1,5},{3,7},{5,1},{7,3},{8,12},{10,14},{12... | collective-permute-start | bytes 442376 | tf_op jit(solution)/shard_map/ppermute | solution.py:256
  32.7 7.0 %collective-permute-start.2 = (bf16[2,96,384]{2,1,0:T(8,128)(2,1)S(1)}, bf16[2,96,384]{2,1,0:T(8,128)(2,1)S(1)}, u32[]{:S(2)}, u32[]{:S(2)}) collective-permute-start(bf16[2,96,384]{2,1,0:T(8,128)(2,1)S(1)} %pad_maximum_fusion.refs_0_), channel_id=1, source_target_pairs={{0,2},{2,0},{4,6},{6,4},{1,3},{3,1},{5,7},{7,5},{8,10},{10,8},{12,... | collective-permute-start | bytes 442376 | tf_op jit(solution)/shard_map/ppermute | solution.py:256
  47.2 2.1 %copy-start.4 = (s32[768]{0:T(1024)S(1)}, s32[768]{0:T(1024)}, u32[]{:S(2)}) copy-start(s32[768]{0:T(1024)} %param.8) | copy-start | bytes 9220
  47.2 4.5 %collective-permute-start.5 = (bf16[32,24,384]{2,1,0:T(8,128)(2,1)S(1)}, bf16[32,24,384]{2,1,0:T(8,128)(2,1)S(1)}, u32[]{:S(2)}, u32[]{:S(2)}) collective-permute-start(bf16[32,24,384]{2,1,0:T(8,128)(2,1)S(1)} %shard_map.107), channel_id=1, source_target_pairs={{0,8},{8,0},{1,9},{9,1},{2,10},{10,2},{3,11},{11,3},{4,12},{12,4},... | collective-permute-start | bytes 1769480 | tf_op jit(solution)/shard_map/ppermute | solution.py:256
  54.0 6.7 %collective-permute-start.10 = (bf16[32,24,384]{2,1,0:T(8,128)(2,1)S(1)}, bf16[32,24,384]{2,1,0:T(8,128)(2,1)S(1)}, u32[]{:S(2)}, u32[]{:S(2)}) collective-permute-start(bf16[32,24,384]{2,1,0:T(8,128)(2,1)S(1)} %bitcast.54), channel_id=1, source_target_pairs={{0,8},{8,0},{1,9},{9,1},{2,10},{10,2},{3,11},{11,3},{4,12},{12,4},... | collective-permute-start | bytes 1769480 | tf_op jit(solution)/shard_map/ppermute | solution.py:256
  58.2 11.2 %collective-permute-start.6 = (bf16[4,96,384]{2,1,0:T(8,128)(2,1)S(1)}, bf16[4,96,384]{2,1,0:T(8,128)(2,1)S(1)}, u32[]{:S(2)}, u32[]{:S(2)}) collective-permute-start(bf16[4,96,384]{2,1,0:T(8,128)(2,1)S(1)} %get-tuple-element.23), channel_id=1, source_target_pairs={{0,1},{1,0},{2,3},{3,2},{4,5},{5,4},{6,7},{7,6},{8,9},{9,8},{10,11... | collective-permute-start | bytes 884744 | tf_op jit(solution)/shard_map/ppermute | solution.py:256
  61.7 26.7 %all-to-all-start.1 = ((bf16[32,24,384]{2,1,0:T(8,128)(2,1)}), bf16[32,24,384]{2,1,0:T(8,128)(2,1)S(1)}, u32[]{:S(2)}, u32[]{:S(2)}) async-start(bf16[32,24,384]{2,1,0:T(8,128)(2,1)} %add_convert_fusion), calls=%async_computation.1 | async-start | bytes 1179648 | tf_op jit(solution)/shard_map/all_to_all | solution.py:252
  69.4 15.9 %copy-start = (f32[300,96]{0,1:T(8,128)S(1)}, f32[300,96]{0,1:T(8,128)}, u32[]{:S(2)}) copy-start(f32[300,96]{0,1:T(8,128)} %param.10) | copy-start | bytes 345604
  69.4 15.9 %copy-start.2 = (f32[300,96]{0,1:T(8,128)S(1)}, f32[300,96]{0,1:T(8,128)}, u32[]{:S(2)}) copy-start(f32[300,96]{0,1:T(8,128)} %param.12) | copy-start | bytes 345604
  69.5 19.1 %copy-start.1 = (f32[300,18]{0,1:T(8,128)S(1)}, f32[300,18]{0,1:T(8,128)}, u32[]{:S(2)}) copy-start(f32[300,18]{0,1:T(8,128)} %param.11) | copy-start | bytes 64804
  69.5 19.1 %copy-start.3 = (f32[300,18]{0,1:T(8,128)S(1)}, f32[300,18]{0,1:T(8,128)}, u32[]{:S(2)}) copy-start(f32[300,18]{0,1:T(8,128)} %param.13) | copy-start | bytes 64804
  69.5 10.5 %collective-permute-start.7 = (bf16[96,384]{1,0:T(8,128)(2,1)S(1)}, bf16[96,384]{1,0:T(8,128)(2,1)S(1)}, u32[]{:S(2)}, u32[]{:S(2)}) collective-permute-start(bf16[96,384]{1,0:T(8,128)(2,1)S(1)} %get-tuple-element.32), channel_id=1, source_target_pairs={{0,2},{2,0},{4,6},{6,4},{1,3},{3,1},{5,7},{7,5},{8,10},{10,8},{12,... | collective-permute-start | bytes 221192 | tf_op jit(solution)/shard_map/ppermute | solution.py:256
  73.5 7.5 %collective-permute-start.9 = (bf16[96,384]{1,0:T(8,128)(2,1)S(1)}, bf16[96,384]{1,0:T(8,128)(2,1)S(1)}, u32[]{:S(2)}, u32[]{:S(2)}) collective-permute-start(bf16[96,384]{1,0:T(8,128)(2,1)S(1)} %get-tuple-element.33), channel_id=1, source_target_pairs={{0,6},{2,4},{4,2},{6,0},{1,7},{3,5},{5,3},{7,1},{8,14},{10,12},{12... | collective-permute-start | bytes 221192 | tf_op jit(solution)/shard_map/ppermute | solution.py:256
  77.5 7.8 %collective-permute-start.8 = (bf16[96,384]{1,0:T(8,128)(2,1)S(1)}, bf16[96,384]{1,0:T(8,128)(2,1)S(1)}, u32[]{:S(2)}, u32[]{:S(2)}) collective-permute-start(bf16[96,384]{1,0:T(8,128)(2,1)S(1)} %get-tuple-element.34), channel_id=1, source_target_pairs={{0,4},{2,6},{4,0},{6,2},{1,5},{3,7},{5,1},{7,3},{8,12},{10,14},{12... | collective-permute-start | bytes 221192 | tf_op jit(solution)/shard_map/ppermute | solution.py:256

commit v5 on v4

--- a/solution.py
+++ b/solution.py
@@ -58,8 +58,8 @@
     )(*[pltpu.with_memory_space_constraint(a, pltpu.HBM) for a in (row_marg, row_t, col_t)])
 
 
-def send_kernel(words, total_ref, rest_ref, col_ref, send_ref):
-    total = total_ref[0:1, 0:1] + rest_ref[0:1, 0:1]
+def send_kernel(words, totals_ref, col_ref, send_ref):
+    total = totals_ref[0, 0:1, 0:1] + totals_ref[1, 0:1, 0:1]
     high = total.astype(BF16).astype(F32)
     middle = (total - high).astype(BF16).astype(F32)
     low = total - high - middle
@@ -71,12 +71,12 @@
         send_ref[i] = value
 
 
-def prepare_send(total, rest, col_own, n_chip, words):
+def prepare_send(totals, col_own, n_chip, words):
     return pl.pallas_call(
         functools.partial(send_kernel, words),
         out_shape=jax.ShapeDtypeStruct((n_chip, GROUP, WIDE), BF16),
         compiler_params=PARAMS,
-    )(total, rest, col_own)
+    )(totals, col_own)
 
 
 def group_of(number):
@@ -267,7 +267,7 @@
     row_line, col_line = row_marg.reshape(1, rows), col_marg.reshape(1, cols)
     own, col_own, total = prepare_own(row_marg.reshape(rows // 128, 128), row_emb.T, col_emb.T)
     beside = flip(own, "zl", 1)
-    send = prepare_send(total, flip(total, "core", 1), col_own, n_chip, words)
+    send = prepare_send(lax.all_gather(total, "core", axis=0), col_own, n_chip, words)
     mine = exchange(after(send, beside))
     both = jnp.stack([own, beside])
     row_half = assemble_rows(place, [both] + [flip(both, "x", k) for k in (1, 2, 3)]).reshape(rows, WIDE)

time: 89.9 us -> 89.8 us (level)
  blocking collectives: 0 us -> 1.8 us
  starting transfers between devices: 54.1 us -> 53.2 us
    ppermute x11 -> x10, waiting for transfers between devices: 9.41 us -> 7.1 us  [flip(): lax.ppermute(block, axis, [(i, i ^ mask) for i in range(lax.axis_size(axi...]
    ppermute x11 -> x10, starting transfers between devices: 33.4 us -> 31.2 us  [flip(): lax.ppermute(block, axis, [(i, i ^ mask) for i in range(lax.axis_size(axi...]
    all_gather x0 -> x1, blocking collectives: none -> 1.8 us  [body(): lax.all_gather(total, 'core', axis=0)]
    all_to_all x2, waiting for transfers between devices: 9.19 us -> 10.7 us  [exchange(): return lax.all_to_all(blocks, CHIP_AXES, 0, 0, tiled=True)]
    all_to_all x2, starting transfers between devices: 20.7 us -> 21.9 us  [exchange(): return lax.all_to_all(blocks, CHIP_AXES, 0, 0, tiled=True)]
  transfers between devices with their start and end apart: 13 -> 12, of which waited for: 8 -> 7; matrix products, arithmetic and copies ran while one was open for 2% -> 2% of each run, Pallas kernels for 11% -> 11%
where the time goes in v5:
time: 89.8 us; the launch traced here: 89.2 us
  starting transfers between devices  53.2 us (59%)
  waiting for transfers between devices  17.8 us (20%)
  Pallas kernels  12.8 us (14%)
  other arithmetic  2.69 us (3%)
  blocking collectives  1.8 us (2%)
  between operations  0.9 us (1%)
    ppermute x10, starting transfers between devices, flip(): lax.ppermute(block, axis, [(i, i ^ mask) for i in range(lax.axis_size(axi...  31.2 us
    all_to_all x2, starting transfers between devices, exchange(): return lax.all_to_all(blocks, CHIP_AXES, 0, 0, tiled=True)  21.9 us
    all_to_all x2, waiting for transfers between devices, exchange(): return lax.all_to_all(blocks, CHIP_AXES, 0, 0, tiled=True)  10.7 us
    ppermute x10, waiting for transfers between devices, flip(): lax.ppermute(block, axis, [(i, i ^ mask) for i in range(lax.axis_size(axi...  7.1 us
    pallas_call x2, Pallas kernels, slopes(): pl.pallas_call(functools.partial(slope_kernel, words), in_specs=[pl.Block...  4.77 us
    pallas_call x1, Pallas kernels, cell_tables(): pl.pallas_call(functools.partial(cells_kernel, words), in_specs=[pl.Block...  3.77 us
  transfers between devices with their start and end apart: 12, of which 7 were waited for; matrix products, arithmetic and copies ran while one was open for 2% of the time, Pallas kernels for 11%

profile of v5, /device:TPU:8, one launch (start us, length us, event | category | flops | bytes accessed | tf_op | source)
XLA Modules:
  0.0 89.2 jit_solution(16614857203244626507)
XLA Ops:
  0.6 1.0 %shard_map.102 = (bf16[96,384]{1,0:T(8,128)(2,1)S(1)}, f32[24,384]{1,0:T(8,128)S(1)}, f32[8,128]{1,0:T(8,128)S(1)}) custom-call(s32[6,128]{1,0:T(8,128)} %bitcast.59, f32[96,300]{1,0:T(8,128)} %bitcast.57, f32[18,300]{1,0:T(8,128)} %bitcast.58), custom_call_target="tpu_custom_call" | custom-call | tf_op jit(solution)/shard_map/pallas_call | solution.py:43
  1.6 4.3 %collective-permute-start = (bf16[96,384]{1,0:T(8,128)(2,1)S(1)}, bf16[96,384]{1,0:T(8,128)(2,1)S(1)}, u32[]{:S(2)}, u32[]{:S(2)}) collective-permute-start(bf16[96,384]{1,0:T(8,128)(2,1)S(1)} %get-tuple-element.17), channel_id=1, source_target_pairs={{0,1},{1,0},{2,3},{3,2},{4,5},{5,4},{6,7},{7,6},{8,9},{9,8},{10,11... | collective-permute-start | bytes 221192 | tf_op jit(solution)/shard_map/ppermute | solution.py:256
  5.9 1.8 %all-gather = f32[16,128]{1,0:T(8,128)S(1)} all-gather(f32[8,128]{1,0:T(8,128)S(1)} %get-tuple-element.15), channel_id=2, replica_groups=mesh['zh'=4,'y'=8,'core'=2,'x'=4,'zl'=2] {'core'}, dimensions={0}, use_global_device_ids=true | all-gather | bytes 12288 | tf_op jit(solution)/shard_map/all_gather | solution.py:270
  7.7 0.9 %shard_map.103.refs_0_ = bf16[32,24,384]{2,1,0:T(8,128)(2,1)} custom-call(f32[2,8,128]{2,1,0:T(8,128)S(1)} %bitcast.55, f32[24,384]{1,0:T(8,128)S(1)} %get-tuple-element.16.col_ref), custom_call_target="tpu_custom_call" | custom-call | tf_op jit(solution)/shard_map/pallas_call | solution.py:75
  8.6 0.0 copy-start.5
  8.6 0.0 collective-permute-done.refs_1_
  8.6 15.4 %all-to-all-start = ((bf16[32,24,384]{2,1,0:T(8,128)(2,1)}), bf16[32,24,384]{2,1,0:T(8,128)(2,1)S(1)}, u32[]{:S(2)}, u32[]{:S(2)}) async-start(bf16[32,24,384]{2,1,0:T(8,128)(2,1)} %shard_map.104), calls=%async_computation | async-start | bytes 1179648 | tf_op jit(solution)/shard_map/all_to_all | solution.py:252
  24.1 4.7 %collective-permute-start.3 = (bf16[2,96,384]{2,1,0:T(8,128)(2,1)S(1)}, bf16[2,96,384]{2,1,0:T(8,128)(2,1)S(1)}, u32[]{:S(2)}, u32[]{:S(2)}) collective-permute-start(bf16[2,96,384]{2,1,0:T(8,128)(2,1)S(1)} %pad_maximum_fusion.refs_0_), channel_id=1, source_target_pairs={{0,6},{2,4},{4,2},{6,0},{1,7},{3,5},{5,3},{7,1},{8,14},{10,12},{12... | collective-permute-start | bytes 442376 | tf_op jit(solution)/shard_map/ppermute | solution.py:256
  28.7 2.7 %collective-permute-start.2 = (bf16[2,96,384]{2,1,0:T(8,128)(2,1)S(1)}, bf16[2,96,384]{2,1,0:T(8,128)(2,1)S(1)}, u32[]{:S(2)}, u32[]{:S(2)}) collective-permute-start(bf16[2,96,384]{2,1,0:T(8,128)(2,1)S(1)} %pad_maximum_fusion.refs_0_), channel_id=1, source_target_pairs={{0,4},{2,6},{4,0},{6,2},{1,5},{3,7},{5,1},{7,3},{8,12},{10,14},{12... | collective-permute-start | bytes 442376 | tf_op jit(solution)/shard_map/ppermute | solution.py:256
  31.5 2.4 %collective-permute-start.1 = (bf16[2,96,384]{2,1,0:T(8,128)(2,1)S(1)}, bf16[2,96,384]{2,1,0:T(8,128)(2,1)S(1)}, u32[]{:S(2)}, u32[]{:S(2)}) collective-permute-start(bf16[2,96,384]{2,1,0:T(8,128)(2,1)S(1)} %pad_maximum_fusion.refs_0_), channel_id=1, source_target_pairs={{0,2},{2,0},{4,6},{6,4},{1,3},{3,1},{5,7},{7,5},{8,10},{10,8},{12,... | collective-permute-start | bytes 442376 | tf_op jit(solution)/shard_map/ppermute | solution.py:256
  33.9 0.0 copy-done.5
  33.9 3.8 %shard_map.106 = (s8[1536,768]{1,0:T(32,128)(4,1)S(1)}, bf16[1536,128]{1,0:T(8,128)(2,1)S(1)}) custom-call(s32[1,1152]{1,0:T(1,128)S(1)} %reshape.41.marg_ref, s32[768,1152]{1,0:T(8,128)} %counts_hbm.1), custom_call_target="tpu_custom_call" | custom-call | tf_op jit(solution)/shard_map/pallas_call | solution.py:135
  37.7 0.1 pad_add_fusion.place_ref
  37.8 0.0 collective-permute-done.3.refs_3_
  37.8 0.2 collective-permute-done.2.refs_2_
  38.0 0.5 collective-permute-done.1.refs_1_
  38.5 0.6 shard_map.105
  39.1 6.9 %all-to-all-done.refs_0_ = bf16[32,24,384]{2,1,0:T(8,128)(2,1)S(1)} async-done(((bf16[32,24,384]{2,1,0:T(8,128)(2,1)}), bf16[32,24,384]{2,1,0:T(8,128)(2,1)S(1)}, u32[]{:S(2)}, u32[]{:S(2)}) %all-to-all-start) | async-done | bytes 589856 | tf_op jit(solution)/shard_map/all_to_all | solution.py:252
  46.0 0.0 copy-start.4
  46.0 2.0 %collective-permute-start.4 = (bf16[32,24,384]{2,1,0:T(8,128)(2,1)S(1)}, bf16[32,24,384]{2,1,0:T(8,128)(2,1)S(1)}, u32[]{:S(2)}, u32[]{:S(2)}) collective-permute-start(bf16[32,24,384]{2,1,0:T(8,128)(2,1)S(1)} %shard_map.107), channel_id=1, source_target_pairs={{0,8},{8,0},{1,9},{9,1},{2,10},{10,2},{3,11},{11,3},{4,12},{12,4},... | collective-permute-start | bytes 1769480 | tf_op jit(solution)/shard_map/ppermute | solution.py:256
  48.0 0.0 copy-done.4
  48.0 2.4 %shard_map.108 = (bf16[768,768]{1,0:T(8,128)(2,1)S(1)}, f32[768,384]{1,0:T(8,128)S(1)}) custom-call(s32[1]{0:T(128)} %bitcast.3.half_ref, bf16[768,384]{1,0:T(8,128)(2,1)S(1)} %bitcast.42, bf16[768,384]{1,0:T(8,128)(2,1)S(1)} %bitcast.43, bf16[768,384]{1,0:T(8,128)(2,1)S(1)} %bitcast.44, bf16[768,384]{1,0:T(8,128)(2,1)S(1)} %bitcast.48, ...), custom_call_target="tpu_custom_call" | custom-call | tf_op jit(solution)/shard_map/pallas_call | solution.py:196
  50.4 0.0 collective-permute-done.4
  50.4 2.4 %shard_map.109 = (bf16[768,768]{1,0:T(8,128)(2,1)S(1)}, bf16[768,384]{1,0:T(8,128)(2,1)S(1)}) custom-call(s32[1]{0:T(128)} %bitcast.12.half_ref, bf16[768,768]{1,0:T(8,128)(2,1)S(1)} %get-tuple-element.20.order_ref.keep_slope_ref, bf16[768,384]{1,0:T(8,128)(2,1)S(1)} %bitcast.50, bf16[768,384]{1,0:T(8,128)(2,1)S(1)} %bitcast.45, ...), custom_call_target="tpu_custom_call" | custom-call | tf_op jit(solution)/shard_map/pallas_call | solution.py:196
  52.8 2.4 %collective-permute-start.9 = (bf16[32,24,384]{2,1,0:T(8,128)(2,1)S(1)}, bf16[32,24,384]{2,1,0:T(8,128)(2,1)S(1)}, u32[]{:S(2)}, u32[]{:S(2)}) collective-permute-start(bf16[32,24,384]{2,1,0:T(8,128)(2,1)S(1)} %bitcast.56), channel_id=1, source_target_pairs={{0,8},{8,0},{1,9},{9,1},{2,10},{10,2},{3,11},{11,3},{4,12},{12,4},... | collective-permute-start | bytes 1769480 | tf_op jit(solution)/shard_map/ppermute | solution.py:256
  55.3 1.7 %shard_map.110 = (f32[4,96,384]{2,1,0:T(8,128)S(1)}, bf16[4,96,384]{2,1,0:T(8,128)(2,1)S(1)}) custom-call(s32[3]{0:T(128)S(1)} %pad_add_fusion.place_ref, bf16[768,384]{1,0:T(8,128)(2,1)S(1)} %bitcast.46, bf16[768,384]{1,0:T(8,128)(2,1)S(1)} %bitcast.51, bf16[768,768]{1,0:T(8,128)(2,1)S(1)} %get-tuple-element.20.order_ref.keep_slope_ref, ...), custom_call_target="tpu_custom_call" | custom-call | tf_op jit(solution)/shard_map/pallas_call | solution.py:222
  57.0 2.4 %collective-permute-start.5 = (bf16[4,96,384]{2,1,0:T(8,128)(2,1)S(1)}, bf16[4,96,384]{2,1,0:T(8,128)(2,1)S(1)}, u32[]{:S(2)}, u32[]{:S(2)}) collective-permute-start(bf16[4,96,384]{2,1,0:T(8,128)(2,1)S(1)} %get-tuple-element.23), channel_id=1, source_target_pairs={{0,1},{1,0},{2,3},{3,2},{4,5},{5,4},{6,7},{7,6},{8,9},{9,8},{10,11... | collective-permute-start | bytes 884744 | tf_op jit(solution)/shard_map/ppermute | solution.py:256
  59.4 0.0 collective-permute-done.9
  59.4 1.0 %add_convert_fusion = bf16[32,24,384]{2,1,0:T(8,128)(2,1)} fusion(f32[32,24,384]{2,1,0:T(8,128)S(1)} %bitcast.52, bf16[32,24,384]{2,1,0:T(8,128)(2,1)S(1)} %collective-permute-done.9), kind=kLoop, calls=%fused_computation.1 | loop fusion | flops 884736 | bytes 2359296 | tf_op jit(solution)/shard_map/convert_element_type | solution.py:284
  60.4 6.5 %all-to-all-start.1 = ((bf16[32,24,384]{2,1,0:T(8,128)(2,1)}), bf16[32,24,384]{2,1,0:T(8,128)(2,1)S(1)}, u32[]{:S(2)}, u32[]{:S(2)}) async-start(bf16[32,24,384]{2,1,0:T(8,128)(2,1)} %add_convert_fusion), calls=%async_computation.1 | async-start | bytes 1179648 | tf_op jit(solution)/shard_map/all_to_all | solution.py:252
  67.0 1.2 %collective-permute-done.5 = bf16[4,96,384]{2,1,0:T(8,128)(2,1)S(1)} collective-permute-done((bf16[4,96,384]{2,1,0:T(8,128)(2,1)S(1)}, bf16[4,96,384]{2,1,0:T(8,128)(2,1)S(1)}, u32[]{:S(2)}, u32[]{:S(2)}) %collective-permute-start.5) | collective-permute-done | bytes 294944 | tf_op jit(solution)/shard_map/ppermute | solution.py:256
  68.2 0.1 fusion.6
  68.3 0.0 copy-start.1
  68.3 0.0 copy-start.3
  68.3 3.7 %collective-permute-start.6 = (bf16[96,384]{1,0:T(8,128)(2,1)S(1)}, bf16[96,384]{1,0:T(8,128)(2,1)S(1)}, u32[]{:S(2)}, u32[]{:S(2)}) collective-permute-start(bf16[96,384]{1,0:T(8,128)(2,1)S(1)} %get-tuple-element.32), channel_id=1, source_target_pairs={{0,2},{2,0},{4,6},{6,4},{1,3},{3,1},{5,7},{7,5},{8,10},{10,8},{12,... | collective-permute-start | bytes 221192 | tf_op jit(solution)/shard_map/ppermute | solution.py:256
  72.1 4.0 %collective-permute-start.8 = (bf16[96,384]{1,0:T(8,128)(2,1)S(1)}, bf16[96,384]{1,0:T(8,128)(2,1)S(1)}, u32[]{:S(2)}, u32[]{:S(2)}) collective-permute-start(bf16[96,384]{1,0:T(8,128)(2,1)S(1)} %get-tuple-element.33), channel_id=1, source_target_pairs={{0,6},{2,4},{4,2},{6,0},{1,7},{3,5},{5,3},{7,1},{8,14},{10,12},{12... | collective-permute-start | bytes 221192 | tf_op jit(solution)/shard_map/ppermute | solution.py:256
  76.1 2.6 %collective-permute-start.7 = (bf16[96,384]{1,0:T(8,128)(2,1)S(1)}, bf16[96,384]{1,0:T(8,128)(2,1)S(1)}, u32[]{:S(2)}, u32[]{:S(2)}) collective-permute-start(bf16[96,384]{1,0:T(8,128)(2,1)S(1)} %get-tuple-element.34), channel_id=1, source_target_pairs={{0,4},{2,6},{4,0},{6,2},{1,5},{3,7},{5,1},{7,3},{8,12},{10,14},{12... | collective-permute-start | bytes 221192 | tf_op jit(solution)/shard_map/ppermute | solution.py:256
  78.7 0.0 collective-permute-done.6
  78.7 0.8 collective-permute-done.8
  79.6 4.3 %collective-permute-done.7 = bf16[96,384]{1,0:T(8,128)(2,1)S(1)} collective-permute-done((bf16[96,384]{1,0:T(8,128)(2,1)S(1)}, bf16[96,384]{1,0:T(8,128)(2,1)S(1)}, u32[]{:S(2)}, u32[]{:S(2)}) %collective-permute-start.7) | collective-permute-done | bytes 73760 | tf_op jit(solution)/shard_map/ppermute | solution.py:256
  83.9 0.0 copy-done
  83.9 0.0 copy-done.2
  83.9 0.8 fusion.2
  84.6 3.8 %all-to-all-done.1 = bf16[32,24,384]{2,1,0:T(8,128)(2,1)S(1)} async-done(((bf16[32,24,384]{2,1,0:T(8,128)(2,1)}), bf16[32,24,384]{2,1,0:T(8,128)(2,1)S(1)}, u32[]{:S(2)}, u32[]{:S(2)}) %all-to-all-start.1) | async-done | bytes 589856 | tf_op jit(solution)/shard_map/all_to_all | solution.py:252
  88.4 0.1 convert_reduce_fusion
  88.5 0.0 copy-done.1
  88.6 0.0 copy-done.3
  88.6 0.6 fusion.4
  (9 shorter events, 0.1 us)
Async XLA Ops:
  1.6 7.0 %collective-permute-start = (bf16[96,384]{1,0:T(8,128)(2,1)S(1)}, bf16[96,384]{1,0:T(8,128)(2,1)S(1)}, u32[]{:S(2)}, u32[]{:S(2)}) collective-permute-start(bf16[96,384]{1,0:T(8,128)(2,1)S(1)} %get-tuple-element.17), channel_id=1, source_target_pairs={{0,1},{1,0},{2,3},{3,2},{4,5},{5,4},{6,7},{7,6},{8,9},{9,8},{10,11... | collective-permute-start | bytes 221192 | tf_op jit(solution)/shard_map/ppermute | solution.py:256
  8.6 25.3 %copy-start.5 = (s32[1152]{0:T(1024)S(1)}, s32[1152]{0:T(1024)}, u32[]{:S(2)}) copy-start(s32[1152]{0:T(1024)} %param.9) | copy-start | bytes 13828
  8.6 37.3 %all-to-all-start = ((bf16[32,24,384]{2,1,0:T(8,128)(2,1)}), bf16[32,24,384]{2,1,0:T(8,128)(2,1)S(1)}, u32[]{:S(2)}, u32[]{:S(2)}) async-start(bf16[32,24,384]{2,1,0:T(8,128)(2,1)} %shard_map.104), calls=%async_computation | async-start | bytes 1179648 | tf_op jit(solution)/shard_map/all_to_all | solution.py:252
  24.1 13.7 %collective-permute-start.3 = (bf16[2,96,384]{2,1,0:T(8,128)(2,1)S(1)}, bf16[2,96,384]{2,1,0:T(8,128)(2,1)S(1)}, u32[]{:S(2)}, u32[]{:S(2)}) collective-permute-start(bf16[2,96,384]{2,1,0:T(8,128)(2,1)S(1)} %pad_maximum_fusion.refs_0_), channel_id=1, source_target_pairs={{0,6},{2,4},{4,2},{6,0},{1,7},{3,5},{5,3},{7,1},{8,14},{10,12},{12... | collective-permute-start | bytes 442376 | tf_op jit(solution)/shard_map/ppermute | solution.py:256
  28.7 9.3 %collective-permute-start.2 = (bf16[2,96,384]{2,1,0:T(8,128)(2,1)S(1)}, bf16[2,96,384]{2,1,0:T(8,128)(2,1)S(1)}, u32[]{:S(2)}, u32[]{:S(2)}) collective-permute-start(bf16[2,96,384]{2,1,0:T(8,128)(2,1)S(1)} %pad_maximum_fusion.refs_0_), channel_id=1, source_target_pairs={{0,4},{2,6},{4,0},{6,2},{1,5},{3,7},{5,1},{7,3},{8,12},{10,14},{12... | collective-permute-start | bytes 442376 | tf_op jit(solution)/shard_map/ppermute | solution.py:256
  31.5 7.0 %collective-permute-start.1 = (bf16[2,96,384]{2,1,0:T(8,128)(2,1)S(1)}, bf16[2,96,384]{2,1,0:T(8,128)(2,1)S(1)}, u32[]{:S(2)}, u32[]{:S(2)}) collective-permute-start(bf16[2,96,384]{2,1,0:T(8,128)(2,1)S(1)} %pad_maximum_fusion.refs_0_), channel_id=1, source_target_pairs={{0,2},{2,0},{4,6},{6,4},{1,3},{3,1},{5,7},{7,5},{8,10},{10,8},{12,... | collective-permute-start | bytes 442376 | tf_op jit(solution)/shard_map/ppermute | solution.py:256
  46.0 2.1 %copy-start.4 = (s32[768]{0:T(1024)S(1)}, s32[768]{0:T(1024)}, u32[]{:S(2)}) copy-start(s32[768]{0:T(1024)} %param.8) | copy-start | bytes 9220
  46.0 4.5 %collective-permute-start.4 = (bf16[32,24,384]{2,1,0:T(8,128)(2,1)S(1)}, bf16[32,24,384]{2,1,0:T(8,128)(2,1)S(1)}, u32[]{:S(2)}, u32[]{:S(2)}) collective-permute-start(bf16[32,24,384]{2,1,0:T(8,128)(2,1)S(1)} %shard_map.107), channel_id=1, source_target_pairs={{0,8},{8,0},{1,9},{9,1},{2,10},{10,2},{3,11},{11,3},{4,12},{12,4},... | collective-permute-start | bytes 1769480 | tf_op jit(solution)/shard_map/ppermute | solution.py:256
  52.8 6.6 %collective-permute-start.9 = (bf16[32,24,384]{2,1,0:T(8,128)(2,1)S(1)}, bf16[32,24,384]{2,1,0:T(8,128)(2,1)S(1)}, u32[]{:S(2)}, u32[]{:S(2)}) collective-permute-start(bf16[32,24,384]{2,1,0:T(8,128)(2,1)S(1)} %bitcast.56), channel_id=1, source_target_pairs={{0,8},{8,0},{1,9},{9,1},{2,10},{10,2},{3,11},{11,3},{4,12},{12,4},... | collective-permute-start | bytes 1769480 | tf_op jit(solution)/shard_map/ppermute | solution.py:256
  57.0 11.2 %collective-permute-start.5 = (bf16[4,96,384]{2,1,0:T(8,128)(2,1)S(1)}, bf16[4,96,384]{2,1,0:T(8,128)(2,1)S(1)}, u32[]{:S(2)}, u32[]{:S(2)}) collective-permute-start(bf16[4,96,384]{2,1,0:T(8,128)(2,1)S(1)} %get-tuple-element.23), channel_id=1, source_target_pairs={{0,1},{1,0},{2,3},{3,2},{4,5},{5,4},{6,7},{7,6},{8,9},{9,8},{10,11... | collective-permute-start | bytes 884744 | tf_op jit(solution)/shard_map/ppermute | solution.py:256
  60.4 28.0 %all-to-all-start.1 = ((bf16[32,24,384]{2,1,0:T(8,128)(2,1)}), bf16[32,24,384]{2,1,0:T(8,128)(2,1)S(1)}, u32[]{:S(2)}, u32[]{:S(2)}) async-start(bf16[32,24,384]{2,1,0:T(8,128)(2,1)} %add_convert_fusion), calls=%async_computation.1 | async-start | bytes 1179648 | tf_op jit(solution)/shard_map/all_to_all | solution.py:252
  68.2 15.7 %copy-start = (f32[300,96]{0,1:T(8,128)S(1)}, f32[300,96]{0,1:T(8,128)}, u32[]{:S(2)}) copy-start(f32[300,96]{0,1:T(8,128)} %param.10) | copy-start | bytes 345604
  68.2 15.7 %copy-start.2 = (f32[300,96]{0,1:T(8,128)S(1)}, f32[300,96]{0,1:T(8,128)}, u32[]{:S(2)}) copy-start(f32[300,96]{0,1:T(8,128)} %param.12) | copy-start | bytes 345604
  68.3 20.3 %copy-start.1 = (f32[300,18]{0,1:T(8,128)S(1)}, f32[300,18]{0,1:T(8,128)}, u32[]{:S(2)}) copy-start(f32[300,18]{0,1:T(8,128)} %param.11) | copy-start | bytes 64804
  68.3 20.3 %copy-start.3 = (f32[300,18]{0,1:T(8,128)S(1)}, f32[300,18]{0,1:T(8,128)}, u32[]{:S(2)}) copy-start(f32[300,18]{0,1:T(8,128)} %param.13) | copy-start | bytes 64804
  68.3 10.4 %collective-permute-start.6 = (bf16[96,384]{1,0:T(8,128)(2,1)S(1)}, bf16[96,384]{1,0:T(8,128)(2,1)S(1)}, u32[]{:S(2)}, u32[]{:S(2)}) collective-permute-start(bf16[96,384]{1,0:T(8,128)(2,1)S(1)} %get-tuple-element.32), channel_id=1, source_target_pairs={{0,2},{2,0},{4,6},{6,4},{1,3},{3,1},{5,7},{7,5},{8,10},{10,8},{12,... | collective-permute-start | bytes 221192 | tf_op jit(solution)/shard_map/ppermute | solution.py:256
  72.1 7.5 %collective-permute-start.8 = (bf16[96,384]{1,0:T(8,128)(2,1)S(1)}, bf16[96,384]{1,0:T(8,128)(2,1)S(1)}, u32[]{:S(2)}, u32[]{:S(2)}) collective-permute-start(bf16[96,384]{1,0:T(8,128)(2,1)S(1)} %get-tuple-element.33), channel_id=1, source_target_pairs={{0,6},{2,4},{4,2},{6,0},{1,7},{3,5},{5,3},{7,1},{8,14},{10,12},{12... | collective-permute-start | bytes 221192 | tf_op jit(solution)/shard_map/ppermute | solution.py:256
  76.1 7.8 %collective-permute-start.7 = (bf16[96,384]{1,0:T(8,128)(2,1)S(1)}, bf16[96,384]{1,0:T(8,128)(2,1)S(1)}, u32[]{:S(2)}, u32[]{:S(2)}) collective-permute-start(bf16[96,384]{1,0:T(8,128)(2,1)S(1)} %get-tuple-element.34), channel_id=1, source_target_pairs={{0,4},{2,6},{4,0},{6,2},{1,5},{3,7},{5,1},{7,3},{8,12},{10,14},{12... | collective-permute-start | bytes 221192 | tf_op jit(solution)/shard_map/ppermute | solution.py:256
